TPU v7x, 512 devices: a whole 4x4x16 slice. The times are simulated.
512 devices in a mesh: row: 16 (over x, y), col: 32 (over z, core).
Axes of the slice: x: 4, y: 4, z: 16, core: 2. Of those that a mesh axis runs over, the one named last changes fastest.
Arguments:
- classes: int32 [256, 4096], P('row', 'col'), may hold values from 0 to 15
- check_index: int32 [1], replicated, may hold values from 8 to 64
- saved_snapshot: bfloat16 [24, 256, 4096], P(None, 'row', 'col'), may hold values from -8 to 8
- payoff_map: bfloat16 [24, 256, 4096], P(None, 'row', 'col'), may hold values from -120 to 160
- final_sensitivity: bfloat16 [24, 256, 4096], P(None, 'row', 'col'), may hold values from -36 to 36
- embed: bfloat16 [16, 64], replicated, may hold values from -6 to 6
- time_vec: bfloat16 [64], replicated, may hold values from -6 to 6
- w_one: bfloat16 [64, 64], replicated, may hold values from -0.75 to 0.75
- w_two: bfloat16 [64, 64], replicated, may hold values from -0.75 to 0.75
- w_three: bfloat16 [64, 24], replicated, may hold values from -0.75 to 0.75
Outputs:
- snapshot_sensitivity: bfloat16 [24, 256, 4096], P(None, 'row', 'col')
- payoff_sensitivity: bfloat16 [24, 256, 4096], P(None, 'row', 'col')
- d_embed: float32 [16, 64], replicated
- d_time: float32 [64], replicated
- d_w_one: float32 [64, 64], replicated
- d_w_two: float32 [64, 64], replicated
- d_w_three: float32 [64, 24], replicated
All inputs are finite; a program needn't handle non-finite values.
Results may differ from a plain program's by a relative error of at most 0.008.
The roundings to bfloat16 on the way count: a program that leaves them out, or rounds other values in their place, can miss the bound.
Values may be sent and summed in bfloat16 or wider, within the bound.
No kernel may reach another device: no remote copies, remote signals or barrier semaphores. Data moves between devices by JAX's collectives and lax.ppermute only.
A program may use at most 64 MiB of HBM per device.

v0:
```python
import math

import jax
import jax.numpy as jnp
from jax import lax
from jax.sharding import PartitionSpec as P

ITERS = 3
CHOICE_NUMBER = 4
STENCIL_POINTS = 5


DECAY_FACTOR = 0.9
SLACK = 0.05


def padded(array, sides, width):
    for axis, dim in sides:
        size, length = (lax.axis_size(axis), array.shape[dim])
        up = [(i, (i + 1) % size) for i in range(size - 1)]
        down = [(j, i) for i, j in up]
        last = lax.slice_in_dim(array, length - width, length, axis=dim)
        first = lax.slice_in_dim(array, 0, width, axis=dim)
        before = lax.ppermute(last, axis, up)
        after = lax.ppermute(first, axis, down)
        array = jnp.concatenate([before, array, after], axis=dim)
    return array


def project(weight_matrix, data_rows):
    return lax.dot_general(
        weight_matrix, data_rows, (((0,), (0,)), ((), ())), preferred_element_type=jnp.float32
    )


def contract_cells(first_part, second_part):
    return lax.dot_general(
        first_part, second_part, (((1,), (1,)), ((), ())), preferred_element_type=jnp.float32
    )


def network_forward(class_ids, index_scale, embed, time_vec, w_one, w_two, w_three):
    one_hot = (jnp.arange(embed.shape[0], dtype=jnp.int32)[:, None] == class_ids[None, :]).astype(
        jnp.bfloat16
    )
    looked = project(embed, one_hot)
    feature = (looked + index_scale * time_vec.astype(jnp.float32)[:, None]).astype(jnp.bfloat16)
    hidden_one = jnp.tanh(project(w_one, feature)).astype(jnp.bfloat16)
    hidden_two = jnp.tanh(project(w_two, hidden_one)).astype(jnp.bfloat16)
    transition_scores = project(w_three, hidden_two)
    return (one_hot, feature, hidden_one, hidden_two, transition_scores)


def blend_weights(transition_scores, widened_height, widened_breadth):
    raw_scores = transition_scores[: CHOICE_NUMBER * STENCIL_POINTS].reshape(
        CHOICE_NUMBER, STENCIL_POINTS, widened_height, widened_breadth
    )
    weights = jax.nn.softplus(raw_scores) + SLACK
    normalizer_sums = jnp.sum(weights, axis=1, keepdims=True)
    transition_chances = weights / normalizer_sums
    choice_payoff_extra = transition_scores[CHOICE_NUMBER * STENCIL_POINTS :].reshape(
        CHOICE_NUMBER, widened_height, widened_breadth
    )
    return (raw_scores, normalizer_sums, transition_chances, choice_payoff_extra)


def crop_flat(field, widened_height, widened_breadth):
    shaped = field.reshape(field.shape[0], widened_height, widened_breadth)
    return shaped.reshape(field.shape[0], -1)


def neighbours(bordered_worths):
    return (
        bordered_worths[:, 1:-1, 1:-1],
        bordered_worths[:, :-2, 1:-1],
        bordered_worths[:, 2:, 1:-1],
        bordered_worths[:, 1:-1, :-2],
        bordered_worths[:, 1:-1, 2:],
    )


def collect_pushed(pushed):
    return (
        pushed[0][:, 1:-1, 1:-1]
        + pushed[1][:, 2:, 1:-1]
        + pushed[2][:, :-2, 1:-1]
        + pushed[3][:, 1:-1, 2:]
        + pushed[4][:, 1:-1, :-2]
    )


def smooth_bellman_update(bordered_worths, transition_chances, choice_payoff_extra, site_payoff):
    nearby = neighbours(bordered_worths)
    scattered_worths = transition_chances[None, :, 0] * nearby[0][:, None]
    for direction in range(1, STENCIL_POINTS):
        scattered_worths = (
            scattered_worths + transition_chances[None, :, direction] * nearby[direction][:, None]
        )
    quality_table = (
        site_payoff[:, None] + choice_payoff_extra[None] + DECAY_FACTOR * scattered_worths
    )
    highest = jnp.max(quality_table, axis=1)
    following_worth = highest + jnp.log(jnp.sum(jnp.exp(quality_table - highest[:, None]), axis=1))
    return (quality_table, following_worth)


def score_sensitivities(
    chance_sensitivity, extra_payoff_sensitivity, raw_scores, normalizer_sums, transition_chances
):
    weighted = jnp.sum(chance_sensitivity * transition_chances, axis=1, keepdims=True)
    raw_sensitivity = (chance_sensitivity - weighted) / normalizer_sums * jax.nn.sigmoid(raw_scores)
    lattice_sites = extra_payoff_sensitivity.shape[1] * extra_payoff_sensitivity.shape[2]
    merged_worths = jnp.concatenate(
        [
            raw_sensitivity.reshape(CHOICE_NUMBER * STENCIL_POINTS, lattice_sites),
            extra_payoff_sensitivity.reshape(CHOICE_NUMBER, lattice_sites),
        ],
        axis=0,
    )
    return merged_worths.astype(jnp.bfloat16)


def network_backward(
    one_hot, feature, hidden_one, hidden_two, score_sensitivity, index_scale, w_one, w_two, w_three
):
    grad_three = contract_cells(hidden_two, score_sensitivity)
    two_f = hidden_two.astype(jnp.float32)
    two_grad = (
        jnp.dot(w_three, score_sensitivity, preferred_element_type=jnp.float32)
        * (1.0 - two_f * two_f)
    ).astype(jnp.bfloat16)
    grad_two = contract_cells(hidden_one, two_grad)
    one_f = hidden_one.astype(jnp.float32)
    one_grad = (
        jnp.dot(w_two, two_grad, preferred_element_type=jnp.float32) * (1.0 - one_f * one_f)
    ).astype(jnp.bfloat16)
    grad_one = contract_cells(feature, one_grad)
    feature_grad = jnp.dot(w_one, one_grad, preferred_element_type=jnp.float32).astype(jnp.bfloat16)
    grad_embed = contract_cells(one_hot, feature_grad)
    grad_time = index_scale * jnp.sum(feature_grad, axis=1, dtype=jnp.float32)
    return (grad_embed, grad_time, grad_one, grad_two, grad_three)


def body(
    classes,
    check_index,
    saved_snapshot,
    payoff_map,
    final_sensitivity,
    embed,
    time_vec,
    w_one,
    w_two,
    w_three,
):
    groups, height_lines, width_cells = saved_snapshot.shape
    index_scale = check_index[0].astype(jnp.float32) / 64.0
    start_field = saved_snapshot.astype(jnp.float32)
    payoff_lattice = payoff_map.astype(jnp.float32)
    worth_sensitivity = final_sensitivity.astype(jnp.float32)
    widened_height, widened_breadth = classes.shape
    one_hot, feature, hidden_one, hidden_two, transition_scores = network_forward(
        classes.reshape(-1), index_scale, embed, time_vec, w_one, w_two, w_three
    )
    raw_scores, normalizer_sums, transition_chances, choice_payoff_extra = blend_weights(
        transition_scores, widened_height, widened_breadth
    )
    stored = []
    present_worth = start_field
    for iteration in range(ITERS):
        bordered_worths = padded(present_worth, (("row", 1), ("col", 2)), 1)
        stored.append(bordered_worths)
        present_worth = smooth_bellman_update(
            bordered_worths, transition_chances, choice_payoff_extra, payoff_lattice
        )[1]
    chance_sensitivity = jnp.zeros(
        (CHOICE_NUMBER, STENCIL_POINTS, height_lines, width_cells), jnp.float32
    )
    extra_payoff_sensitivity = jnp.zeros((CHOICE_NUMBER, height_lines, width_cells), jnp.float32)
    payoff_site_sensitivity = jnp.zeros((groups, height_lines, width_cells), jnp.float32)
    for iteration in reversed(range(ITERS)):
        bordered_worths = stored[iteration]
        quality_table, following_worth = smooth_bellman_update(
            bordered_worths, transition_chances, choice_payoff_extra, payoff_lattice
        )
        quality_sensitivity = worth_sensitivity[:, None] * jnp.exp(
            quality_table - following_worth[:, None]
        )
        payoff_site_sensitivity = payoff_site_sensitivity + jnp.sum(quality_sensitivity, axis=1)
        extra_payoff_sensitivity = extra_payoff_sensitivity + jnp.sum(quality_sensitivity, axis=0)
        nearby_own = neighbours(bordered_worths)
        chance_sensitivity = chance_sensitivity + DECAY_FACTOR * jnp.stack(
            [
                jnp.sum(quality_sensitivity * nearby_own[direction][:, None], axis=0)
                for direction in range(STENCIL_POINTS)
            ],
            axis=1,
        )
        pushed = [
            DECAY_FACTOR
            * jnp.sum(quality_sensitivity * transition_chances[None, :, direction], axis=1)
            for direction in range(STENCIL_POINTS)
        ]
        worth_sensitivity = collect_pushed(
            [jnp.pad(piece, ((0, 0), (1, 1), (1, 1))) for piece in pushed]
        )
        row_edges = jnp.stack([pushed[1][:, 0, :], pushed[2][:, -1, :]], axis=1)
        from_rows = padded(row_edges, (("row", 1),), 1)
        col_edges = jnp.stack([pushed[3][:, :, 0], pushed[4][:, :, -1]], axis=2)
        from_cols = padded(col_edges, (("col", 2),), 1)
        worth_sensitivity = (
            worth_sensitivity.at[:, 0, :]
            .add(from_rows[:, 0, :])
            .at[:, -1, :]
            .add(from_rows[:, 3, :])
        )
        worth_sensitivity = (
            worth_sensitivity.at[:, :, 0]
            .add(from_cols[:, :, 0])
            .at[:, :, -1]
            .add(from_cols[:, :, 3])
        )
    snapshot_sensitivity = worth_sensitivity.astype(jnp.bfloat16)
    payoff_sensitivity = payoff_site_sensitivity.astype(jnp.bfloat16)
    score_sensitivity = score_sensitivities(
        chance_sensitivity,
        extra_payoff_sensitivity,
        raw_scores,
        normalizer_sums,
        transition_chances,
    )
    gradients = network_backward(
        crop_flat(one_hot, widened_height, widened_breadth),
        crop_flat(feature, widened_height, widened_breadth),
        crop_flat(hidden_one, widened_height, widened_breadth),
        crop_flat(hidden_two, widened_height, widened_breadth),
        score_sensitivity,
        index_scale,
        w_one,
        w_two,
        w_three,
    )
    summed = lax.psum(
        (gradients[0], gradients[1], gradients[2], gradients[3], gradients[4]), ("row", "col")
    )
    grad_scale = 1.0 / math.sqrt(
        height_lines * lax.axis_size("row") * width_cells * lax.axis_size("col")
    )
    return (
        snapshot_sensitivity,
        payoff_sensitivity,
        summed[0] * grad_scale,
        summed[1] * grad_scale,
        summed[2] * grad_scale,
        summed[3] * grad_scale,
        summed[4] * grad_scale,
    )


def solution(mesh):
    return jax.shard_map(
        body,
        mesh=mesh,
        in_specs=(
            P("row", "col"),
            P(),
            P(None, "row", "col"),
            P(None, "row", "col"),
            P(None, "row", "col"),
            P(),
            P(),
            P(),
            P(),
            P(),
        ),
        out_specs=(P(None, "row", "col"), P(None, "row", "col"), P(), P(), P(), P(), P()),
        check_vma=False,
    )
```

profile of v0, /device:TPU:1, one launch (start us, length us, event | category | flops | bytes accessed | tf_op | source)
XLA Modules:
  0.0 259.6 jit_solution(16986548333126786515)
XLA Ops:
  1.5 4.0 %collective-permute-start = (f32[24,1,128]{2,1,0:T(1,128)S(1)}, f32[24,1,128]{2,1,0:T(1,128)S(1)}, u32[]{:S(2)}, u32[]{:S(2)}) collective-permute-start(f32[24,1,128]{2,1,0:T(1,128)S(1)} %get-tuple-element.219), channel_id=1, source_target_pairs={{0,32},{32,64},{64,96},{96,128},{128,160},{160,192},{192,224},{224... | collective-permute-start | bytes 36872 | tf_op jit(solution)/shard_map/ppermute | solution.py:24
  11.5 4.4 %collective-permute-start.2 = (f32[24,18,1]{2,1,0:T(8,128)S(1)}, f32[24,18,1]{2,1,0:T(8,128)S(1)}, u32[]{:S(2)}, u32[]{:S(2)}) collective-permute-start(f32[24,18,1]{2,1,0:T(8,128)S(1)} %get-tuple-element.196), channel_id=1, source_target_pairs={{0,1},{1,2},{2,3},{3,4},{4,5},{5,6},{6,7},{7,8},{8,9},{9,10},{10,1... | collective-permute-start | bytes 5192 | tf_op jit(solution)/shard_map/ppermute | solution.py:24
  15.9 3.0 %collective-permute-start.3 = (f32[24,18,1]{2,1,0:T(8,128)S(1)}, f32[24,18,1]{2,1,0:T(8,128)S(1)}, u32[]{:S(2)}, u32[]{:S(2)}) collective-permute-start(f32[24,18,1]{2,1,0:T(8,128)S(1)} %get-tuple-element.197), channel_id=1, source_target_pairs={{1,0},{2,1},{3,2},{4,3},{5,4},{6,5},{7,6},{8,7},{9,8},{10,9},{11,1... | collective-permute-start | bytes 5192 | tf_op jit(solution)/shard_map/ppermute | solution.py:25
  19.6 4.4 %collective-permute-done.3 = f32[24,18,1]{2,1,0:T(8,128)S(1)} collective-permute-done((f32[24,18,1]{2,1,0:T(8,128)S(1)}, f32[24,18,1]{2,1,0:T(8,128)S(1)}, u32[]{:S(2)}, u32[]{:S(2)}) %collective-permute-start.3) | collective-permute-done | bytes 1760 | tf_op jit(solution)/shard_map/ppermute | solution.py:25
  25.2 4.3 %collective-permute-start.4 = (f32[24,1,128]{2,1,0:T(1,128)S(1)}, f32[24,1,128]{2,1,0:T(1,128)S(1)}, u32[]{:S(2)}, u32[]{:S(2)}) collective-permute-start(f32[24,1,128]{2,1,0:T(1,128)S(1)} %get-tuple-element.212), channel_id=1, source_target_pairs={{0,32},{32,64},{64,96},{96,128},{128,160},{160,192},{192,224},{224... | collective-permute-start | bytes 36872 | tf_op jit(solution)/shard_map/ppermute | solution.py:24
  30.8 3.1 %collective-permute-done.5 = f32[24,1,128]{2,1,0:T(1,128)S(1)} collective-permute-done((f32[24,1,128]{2,1,0:T(1,128)S(1)}, f32[24,1,128]{2,1,0:T(1,128)S(1)}, u32[]{:S(2)}, u32[]{:S(2)}) %collective-permute-start.5) | collective-permute-done | bytes 12320 | tf_op jit(solution)/shard_map/ppermute | solution.py:25
  34.1 3.2 %collective-permute-start.6 = (f32[24,18,1]{2,1,0:T(8,128)S(1)}, f32[24,18,1]{2,1,0:T(8,128)S(1)}, u32[]{:S(2)}, u32[]{:S(2)}) collective-permute-start(f32[24,18,1]{2,1,0:T(8,128)S(1)} %get-tuple-element.194), channel_id=1, source_target_pairs={{0,1},{1,2},{2,3},{3,4},{4,5},{5,6},{6,7},{7,8},{8,9},{9,10},{10,1... | collective-permute-start | bytes 5192 | tf_op jit(solution)/shard_map/ppermute | solution.py:24
  40.9 4.4 %collective-permute-done.7 = f32[24,18,1]{2,1,0:T(8,128)S(1)} collective-permute-done((f32[24,18,1]{2,1,0:T(8,128)S(1)}, f32[24,18,1]{2,1,0:T(8,128)S(1)}, u32[]{:S(2)}, u32[]{:S(2)}) %collective-permute-start.7) | collective-permute-done | bytes 1760 | tf_op jit(solution)/shard_map/ppermute | solution.py:25
  46.6 3.2 %collective-permute-start.8 = (f32[24,1,128]{2,1,0:T(1,128)S(1)}, f32[24,1,128]{2,1,0:T(1,128)S(1)}, u32[]{:S(2)}, u32[]{:S(2)}) collective-permute-start(f32[24,1,128]{2,1,0:T(1,128)S(1)} %get-tuple-element.210), channel_id=1, source_target_pairs={{0,32},{32,64},{64,96},{96,128},{128,160},{160,192},{192,224},{224... | collective-permute-start | bytes 36872 | tf_op jit(solution)/shard_map/ppermute | solution.py:24
  51.1 3.9 %collective-permute-done.9 = f32[24,1,128]{2,1,0:T(1,128)S(1)} collective-permute-done((f32[24,1,128]{2,1,0:T(1,128)S(1)}, f32[24,1,128]{2,1,0:T(1,128)S(1)}, u32[]{:S(2)}, u32[]{:S(2)}) %collective-permute-start.9) | collective-permute-done | bytes 12320 | tf_op jit(solution)/shard_map/ppermute | solution.py:25
  55.2 2.9 %collective-permute-start.10 = (f32[24,18,1]{2,1,0:T(8,128)S(1)}, f32[24,18,1]{2,1,0:T(8,128)S(1)}, u32[]{:S(2)}, u32[]{:S(2)}) collective-permute-start(f32[24,18,1]{2,1,0:T(8,128)S(1)} %get-tuple-element.192), channel_id=1, source_target_pairs={{0,1},{1,2},{2,3},{3,4},{4,5},{5,6},{6,7},{7,8},{8,9},{9,10},{10,1... | collective-permute-start | bytes 5192 | tf_op jit(solution)/shard_map/ppermute | solution.py:24
  61.8 4.4 %collective-permute-done.11 = f32[24,18,1]{2,1,0:T(8,128)S(1)} collective-permute-done((f32[24,18,1]{2,1,0:T(8,128)S(1)}, f32[24,18,1]{2,1,0:T(8,128)S(1)}, u32[]{:S(2)}, u32[]{:S(2)}) %collective-permute-start.11) | collective-permute-done | bytes 1760 | tf_op jit(solution)/shard_map/ppermute | solution.py:25
  69.9 5.7 %collective-permute-start.12 = (f32[24,1,128]{2,1,0:T(1,128)S(1)}, f32[24,1,128]{2,1,0:T(1,128)S(1)}, u32[]{:S(2)}, u32[]{:S(2)}) collective-permute-start(f32[24,1,128]{2,1,0:T(1,128)S(1)} %slice.586), channel_id=1, source_target_pairs={{0,32},{32,64},{64,96},{96,128},{128,160},{160,192},{192,224},{224... | collective-permute-start | bytes 36872 | tf_op jit(solution)/shard_map/ppermute | solution.py:24
  77.8 2.0 collective-permute-start.14
  80.9 3.0 %collective-permute-start.15 = (f32[24,16,1]{2,1,0:T(8,128)}, f32[24,16,1]{2,1,0:T(8,128)}, u32[]{:S(2)}, u32[]{:S(2)}) collective-permute-start(f32[24,16,1]{2,1,0:T(8,128)} %bitcast.81), channel_id=1, source_target_pairs={{1,0},{2,1},{3,2},{4,3},{5,4},{6,5},{7,6},{8,7},{9,8},{10,9},{11,1... | collective-permute-start | bytes 4616 | tf_op jit(solution)/shard_map/ppermute | solution.py:25
  90.9 2.7 %scatter-add.45 = f32[24,16,128]{2,1,0:T(8,128)S(1)} dynamic-update-slice(f32[24,16,128]{2,1,0:T(8,128)S(1)} %scatter-add.44, f32[24,16,1]{2,1,0:T(8,128)} %slice_add_fusion.4, s32[]{:T(128)} %constant.293.clone.1, s32[]{:T(128)} %constant.293.clone.1, s32[]{:T(128)} %constant.295.clone.1) | dynamic-update-slice | bytes 3076 | tf_op jit(solution)/shard_map/scatter-add | solution.py:221
  95.4 4.0 %collective-permute-start.16 = (f32[24,1,128]{2,1,0:T(1,128)S(1)}, f32[24,1,128]{2,1,0:T(1,128)S(1)}, u32[]{:S(2)}, u32[]{:S(2)}) collective-permute-start(f32[24,1,128]{2,1,0:T(1,128)S(1)} %slice.594), channel_id=1, source_target_pairs={{0,32},{32,64},{64,96},{96,128},{128,160},{160,192},{192,224},{224... | collective-permute-start | bytes 36872 | tf_op jit(solution)/shard_map/ppermute | solution.py:24
  100.9 2.9 %collective-permute-start.18 = (f32[24,16,1]{2,1,0:T(8,128)S(1)}, f32[24,16,1]{2,1,0:T(8,128)}, u32[]{:S(2)}, u32[]{:S(2)}) collective-permute-start(f32[24,16,1]{2,1,0:T(8,128)S(1)} %slice.598), channel_id=1, source_target_pairs={{0,1},{1,2},{2,3},{3,4},{4,5},{5,6},{6,7},{7,8},{8,9},{9,10},{10,1... | collective-permute-start | bytes 4616 | tf_op jit(solution)/shard_map/ppermute | solution.py:24
  103.9 2.1 collective-permute-start.19
  108.4 4.0 %collective-permute-done.19 = f32[24,16,1]{2,1,0:T(8,128)S(1)} collective-permute-done((f32[24,16,1]{2,1,0:T(8,128)S(1)}, f32[24,16,1]{2,1,0:T(8,128)S(1)}, u32[]{:S(2)}, u32[]{:S(2)}) %collective-permute-start.19) | collective-permute-done | bytes 1568 | tf_op jit(solution)/shard_map/ppermute | solution.py:25
  122.2 117.2 %all-reduce.12 = (f32[16,64]{1,0:T(8,128)S(1)}, f32[64]{0:T(128)S(1)}, f32[64,64]{1,0:T(8,128)S(1)}, f32[64,64]{1,0:T(8,128)S(1)}, f32[64,24]{0,1:T(8,128)S(1)}) all-reduce(f32[16,64]{1,0:T(8,128)S(1)} %fusion.21, f32[64]{0:T(128)S(1)} %broadcast_multiply_fusion.17, ...), channel_id=1, replica_groups=mesh['row'=16,'col'=32] {'row','col'}, use_global_device_ids=true, to_apply=%region_44.45 | all-reduce | flops 10816 | bytes 86528 | tf_op jit(solution)/shard_map/psum | solution.py:243
  242.1 2.8 %collective-permute-start.20 = (f32[24,1,128]{2,1,0:T(1,128)S(1)}, f32[24,1,128]{2,1,0:T(1,128)S(1)}, u32[]{:S(2)}, u32[]{:S(2)}) collective-permute-start(f32[24,1,128]{2,1,0:T(1,128)S(1)} %slice.602), channel_id=1, source_target_pairs={{0,32},{32,64},{64,96},{96,128},{128,160},{160,192},{192,224},{224... | collective-permute-start | bytes 36872 | tf_op jit(solution)/shard_map/ppermute | solution.py:24
  250.0 2.4 collective-permute-start.23
  252.9 4.1 %collective-permute-done.23 = f32[24,16,1]{2,1,0:T(8,128)S(1)} collective-permute-done((f32[24,16,1]{2,1,0:T(8,128)S(1)}, f32[24,16,1]{2,1,0:T(8,128)S(1)}, u32[]{:S(2)}, u32[]{:S(2)}) %collective-permute-start.23) | collective-permute-done | bytes 1568 | tf_op jit(solution)/shard_map/ppermute | solution.py:25
  (195 shorter events, 59.0 us)
Async XLA Ops:
  1.5 9.8 %collective-permute-start = (f32[24,1,128]{2,1,0:T(1,128)S(1)}, f32[24,1,128]{2,1,0:T(1,128)S(1)}, u32[]{:S(2)}, u32[]{:S(2)}) collective-permute-start(f32[24,1,128]{2,1,0:T(1,128)S(1)} %get-tuple-element.219), channel_id=1, source_target_pairs={{0,32},{32,64},{64,96},{96,128},{128,160},{160,192},{192,224},{224... | collective-permute-start | bytes 36872 | tf_op jit(solution)/shard_map/ppermute | solution.py:24
  5.5 5.8 %collective-permute-start.1 = (f32[24,1,128]{2,1,0:T(1,128)S(1)}, f32[24,1,128]{2,1,0:T(1,128)S(1)}, u32[]{:S(2)}, u32[]{:S(2)}) collective-permute-start(f32[24,1,128]{2,1,0:T(1,128)S(1)} %get-tuple-element.220), channel_id=1, source_target_pairs={{32,0},{64,32},{96,64},{128,96},{160,128},{192,160},{224,192},{256... | collective-permute-start | bytes 36872 | tf_op jit(solution)/shard_map/ppermute | solution.py:25
  11.5 8.0 %collective-permute-start.2 = (f32[24,18,1]{2,1,0:T(8,128)S(1)}, f32[24,18,1]{2,1,0:T(8,128)S(1)}, u32[]{:S(2)}, u32[]{:S(2)}) collective-permute-start(f32[24,18,1]{2,1,0:T(8,128)S(1)} %get-tuple-element.196), channel_id=1, source_target_pairs={{0,1},{1,2},{2,3},{3,4},{4,5},{5,6},{6,7},{7,8},{8,9},{9,10},{10,1... | collective-permute-start | bytes 5192 | tf_op jit(solution)/shard_map/ppermute | solution.py:24
  15.9 8.0 %collective-permute-start.3 = (f32[24,18,1]{2,1,0:T(8,128)S(1)}, f32[24,18,1]{2,1,0:T(8,128)S(1)}, u32[]{:S(2)}, u32[]{:S(2)}) collective-permute-start(f32[24,18,1]{2,1,0:T(8,128)S(1)} %get-tuple-element.197), channel_id=1, source_target_pairs={{1,0},{2,1},{3,2},{4,3},{5,4},{6,5},{7,6},{8,7},{9,8},{10,9},{11,1... | collective-permute-start | bytes 5192 | tf_op jit(solution)/shard_map/ppermute | solution.py:25
  25.2 5.6 %collective-permute-start.4 = (f32[24,1,128]{2,1,0:T(1,128)S(1)}, f32[24,1,128]{2,1,0:T(1,128)S(1)}, u32[]{:S(2)}, u32[]{:S(2)}) collective-permute-start(f32[24,1,128]{2,1,0:T(1,128)S(1)} %get-tuple-element.212), channel_id=1, source_target_pairs={{0,32},{32,64},{64,96},{96,128},{128,160},{160,192},{192,224},{224... | collective-permute-start | bytes 36872 | tf_op jit(solution)/shard_map/ppermute | solution.py:24
  29.5 4.4 %collective-permute-start.5 = (f32[24,1,128]{2,1,0:T(1,128)S(1)}, f32[24,1,128]{2,1,0:T(1,128)S(1)}, u32[]{:S(2)}, u32[]{:S(2)}) collective-permute-start(f32[24,1,128]{2,1,0:T(1,128)S(1)} %get-tuple-element.213), channel_id=1, source_target_pairs={{32,0},{64,32},{96,64},{128,96},{160,128},{192,160},{224,192},{256... | collective-permute-start | bytes 36872 | tf_op jit(solution)/shard_map/ppermute | solution.py:25
  34.1 6.8 %collective-permute-start.6 = (f32[24,18,1]{2,1,0:T(8,128)S(1)}, f32[24,18,1]{2,1,0:T(8,128)S(1)}, u32[]{:S(2)}, u32[]{:S(2)}) collective-permute-start(f32[24,18,1]{2,1,0:T(8,128)S(1)} %get-tuple-element.194), channel_id=1, source_target_pairs={{0,1},{1,2},{2,3},{3,4},{4,5},{5,6},{6,7},{7,8},{8,9},{9,10},{10,1... | collective-permute-start | bytes 5192 | tf_op jit(solution)/shard_map/ppermute | solution.py:24
  37.3 8.0 %collective-permute-start.7 = (f32[24,18,1]{2,1,0:T(8,128)S(1)}, f32[24,18,1]{2,1,0:T(8,128)S(1)}, u32[]{:S(2)}, u32[]{:S(2)}) collective-permute-start(f32[24,18,1]{2,1,0:T(8,128)S(1)} %get-tuple-element.195), channel_id=1, source_target_pairs={{1,0},{2,1},{3,2},{4,3},{5,4},{6,5},{7,6},{8,7},{9,8},{10,9},{11,1... | collective-permute-start | bytes 5192 | tf_op jit(solution)/shard_map/ppermute | solution.py:25
  46.6 4.5 %collective-permute-start.8 = (f32[24,1,128]{2,1,0:T(1,128)S(1)}, f32[24,1,128]{2,1,0:T(1,128)S(1)}, u32[]{:S(2)}, u32[]{:S(2)}) collective-permute-start(f32[24,1,128]{2,1,0:T(1,128)S(1)} %get-tuple-element.210), channel_id=1, source_target_pairs={{0,32},{32,64},{64,96},{96,128},{128,160},{160,192},{192,224},{224... | collective-permute-start | bytes 36872 | tf_op jit(solution)/shard_map/ppermute | solution.py:24
  49.8 5.2 %collective-permute-start.9 = (f32[24,1,128]{2,1,0:T(1,128)S(1)}, f32[24,1,128]{2,1,0:T(1,128)S(1)}, u32[]{:S(2)}, u32[]{:S(2)}) collective-permute-start(f32[24,1,128]{2,1,0:T(1,128)S(1)} %get-tuple-element.211), channel_id=1, source_target_pairs={{32,0},{64,32},{96,64},{128,96},{160,128},{192,160},{224,192},{256... | collective-permute-start | bytes 36872 | tf_op jit(solution)/shard_map/ppermute | solution.py:25
  55.2 6.6 %collective-permute-start.10 = (f32[24,18,1]{2,1,0:T(8,128)S(1)}, f32[24,18,1]{2,1,0:T(8,128)S(1)}, u32[]{:S(2)}, u32[]{:S(2)}) collective-permute-start(f32[24,18,1]{2,1,0:T(8,128)S(1)} %get-tuple-element.192), channel_id=1, source_target_pairs={{0,1},{1,2},{2,3},{3,4},{4,5},{5,6},{6,7},{7,8},{8,9},{9,10},{10,1... | collective-permute-start | bytes 5192 | tf_op jit(solution)/shard_map/ppermute | solution.py:24
  58.1 8.0 %collective-permute-start.11 = (f32[24,18,1]{2,1,0:T(8,128)S(1)}, f32[24,18,1]{2,1,0:T(8,128)S(1)}, u32[]{:S(2)}, u32[]{:S(2)}) collective-permute-start(f32[24,18,1]{2,1,0:T(8,128)S(1)} %get-tuple-element.193), channel_id=1, source_target_pairs={{1,0},{2,1},{3,2},{4,3},{5,4},{6,5},{7,6},{8,7},{9,8},{10,9},{11,1... | collective-permute-start | bytes 5192 | tf_op jit(solution)/shard_map/ppermute | solution.py:25
  69.9 14.1 %collective-permute-start.12 = (f32[24,1,128]{2,1,0:T(1,128)S(1)}, f32[24,1,128]{2,1,0:T(1,128)S(1)}, u32[]{:S(2)}, u32[]{:S(2)}) collective-permute-start(f32[24,1,128]{2,1,0:T(1,128)S(1)} %slice.586), channel_id=1, source_target_pairs={{0,32},{32,64},{64,96},{96,128},{128,160},{160,192},{192,224},{224... | collective-permute-start | bytes 36872 | tf_op jit(solution)/shard_map/ppermute | solution.py:24
  76.5 8.2 %collective-permute-start.13 = (f32[24,1,128]{2,1,0:T(1,128)S(1)}, f32[24,1,128]{2,1,0:T(1,128)}, u32[]{:S(2)}, u32[]{:S(2)}) collective-permute-start(f32[24,1,128]{2,1,0:T(1,128)S(1)} %slice.588), channel_id=1, source_target_pairs={{32,0},{64,32},{96,64},{128,96},{160,128},{192,160},{224,192},{256... | collective-permute-start | bytes 36872 | tf_op jit(solution)/shard_map/ppermute | solution.py:25
  77.8 7.8 %collective-permute-start.14 = (f32[24,16,1]{2,1,0:T(8,128)}, f32[24,16,1]{2,1,0:T(8,128)}, u32[]{:S(2)}, u32[]{:S(2)}) collective-permute-start(f32[24,16,1]{2,1,0:T(8,128)} %slice.590), channel_id=1, source_target_pairs={{0,1},{1,2},{2,3},{3,4},{4,5},{5,6},{6,7},{7,8},{8,9},{9,10},{10,1... | collective-permute-start | bytes 4616 | tf_op jit(solution)/shard_map/ppermute | solution.py:24
  80.9 8.2 %collective-permute-start.15 = (f32[24,16,1]{2,1,0:T(8,128)}, f32[24,16,1]{2,1,0:T(8,128)}, u32[]{:S(2)}, u32[]{:S(2)}) collective-permute-start(f32[24,16,1]{2,1,0:T(8,128)} %bitcast.81), channel_id=1, source_target_pairs={{1,0},{2,1},{3,2},{4,3},{5,4},{6,5},{7,6},{8,7},{9,8},{10,9},{11,1... | collective-permute-start | bytes 4616 | tf_op jit(solution)/shard_map/ppermute | solution.py:25
  95.4 10.7 %collective-permute-start.16 = (f32[24,1,128]{2,1,0:T(1,128)S(1)}, f32[24,1,128]{2,1,0:T(1,128)S(1)}, u32[]{:S(2)}, u32[]{:S(2)}) collective-permute-start(f32[24,1,128]{2,1,0:T(1,128)S(1)} %slice.594), channel_id=1, source_target_pairs={{0,32},{32,64},{64,96},{96,128},{128,160},{160,192},{192,224},{224... | collective-permute-start | bytes 36872 | tf_op jit(solution)/shard_map/ppermute | solution.py:24
  99.6 6.7 %collective-permute-start.17 = (f32[24,1,128]{2,1,0:T(1,128)S(1)}, f32[24,1,128]{2,1,0:T(1,128)}, u32[]{:S(2)}, u32[]{:S(2)}) collective-permute-start(f32[24,1,128]{2,1,0:T(1,128)S(1)} %slice.596), channel_id=1, source_target_pairs={{32,0},{64,32},{96,64},{128,96},{160,128},{192,160},{224,192},{256... | collective-permute-start | bytes 36872 | tf_op jit(solution)/shard_map/ppermute | solution.py:25
  100.9 6.2 %collective-permute-start.18 = (f32[24,16,1]{2,1,0:T(8,128)S(1)}, f32[24,16,1]{2,1,0:T(8,128)}, u32[]{:S(2)}, u32[]{:S(2)}) collective-permute-start(f32[24,16,1]{2,1,0:T(8,128)S(1)} %slice.598), channel_id=1, source_target_pairs={{0,1},{1,2},{2,3},{3,4},{4,5},{5,6},{6,7},{7,8},{8,9},{9,10},{10,1... | collective-permute-start | bytes 4616 | tf_op jit(solution)/shard_map/ppermute | solution.py:24
  103.9 8.5 %collective-permute-start.19 = (f32[24,16,1]{2,1,0:T(8,128)S(1)}, f32[24,16,1]{2,1,0:T(8,128)S(1)}, u32[]{:S(2)}, u32[]{:S(2)}) collective-permute-start(f32[24,16,1]{2,1,0:T(8,128)S(1)} %bitcast.98), channel_id=1, source_target_pairs={{1,0},{2,1},{3,2},{4,3},{5,4},{6,5},{7,6},{8,7},{9,8},{10,9},{11,1... | collective-permute-start | bytes 4616 | tf_op jit(solution)/shard_map/ppermute | solution.py:25
  242.1 10.3 %collective-permute-start.20 = (f32[24,1,128]{2,1,0:T(1,128)S(1)}, f32[24,1,128]{2,1,0:T(1,128)S(1)}, u32[]{:S(2)}, u32[]{:S(2)}) collective-permute-start(f32[24,1,128]{2,1,0:T(1,128)S(1)} %slice.602), channel_id=1, source_target_pairs={{0,32},{32,64},{64,96},{96,128},{128,160},{160,192},{192,224},{224... | collective-permute-start | bytes 36872 | tf_op jit(solution)/shard_map/ppermute | solution.py:24
  245.1 7.4 %collective-permute-start.21 = (f32[24,1,128]{2,1,0:T(1,128)S(1)}, f32[24,1,128]{2,1,0:T(1,128)S(1)}, u32[]{:S(2)}, u32[]{:S(2)}) collective-permute-start(f32[24,1,128]{2,1,0:T(1,128)S(1)} %slice.604), channel_id=1, source_target_pairs={{32,0},{64,32},{96,64},{128,96},{160,128},{192,160},{224,192},{256... | collective-permute-start | bytes 36872 | tf_op jit(solution)/shard_map/ppermute | solution.py:25
  246.5 6.1 %collective-permute-start.22 = (f32[24,16,1]{2,1,0:T(8,128)S(1)}, f32[24,16,1]{2,1,0:T(8,128)S(1)}, u32[]{:S(2)}, u32[]{:S(2)}) collective-permute-start(f32[24,16,1]{2,1,0:T(8,128)S(1)} %slice.606), channel_id=1, source_target_pairs={{0,1},{1,2},{2,3},{3,4},{4,5},{5,6},{6,7},{7,8},{8,9},{9,10},{10,1... | collective-permute-start | bytes 4616 | tf_op jit(solution)/shard_map/ppermute | solution.py:24
  250.0 7.0 %collective-permute-start.23 = (f32[24,16,1]{2,1,0:T(8,128)S(1)}, f32[24,16,1]{2,1,0:T(8,128)S(1)}, u32[]{:S(2)}, u32[]{:S(2)}) collective-permute-start(f32[24,16,1]{2,1,0:T(8,128)S(1)} %bitcast.97), channel_id=1, source_target_pairs={{1,0},{2,1},{3,2},{4,3},{5,4},{6,5},{7,6},{8,7},{9,8},{10,9},{11,1... | collective-permute-start | bytes 4616 | tf_op jit(solution)/shard_map/ppermute | solution.py:25
  (23 other events, 178.3 us)
where the time goes:
time: 264 us; the launch traced here: 260 us
  blocking collectives  117 us (44%)
  starting transfers between devices  63.6 us (24%)
  waiting for transfers between devices  33.3 us (13%)
  other arithmetic  21.6 us (8%)
  local copies, waits for them, and re-layouts  18.9 us (7%)
    psum x1, blocking collectives, body(): lax.psum((gradients[0], gradients[1], gradients[2], gradients[3], gradien...  117 us
    ppermute x12, starting transfers between devices, padded(): before = lax.ppermute(last, axis, up)  41.4 us
    ppermute x12, waiting for transfers between devices, padded(): after = lax.ppermute(first, axis, down)  29.3 us
    ppermute x12, starting transfers between devices, padded(): after = lax.ppermute(first, axis, down)  22.2 us
    unnamed x65, local copies, waits for them, and re-layouts  8.01 us
    scatter-add x6, local copies, waits for them, and re-layouts, body(): worth_sensitivity = worth_sensitivity.at[:, :, 0].add(from_cols[:, :, 0])...  7.97 us
    reduce_sum x3, other arithmetic, body(): jnp.sum(quality_sensitivity * nearby_own[direction][:, None], axis=0)  5.3 us
  transfers between devices with their start and end apart: 24, of which 11 were waited for; matrix products, arithmetic and copies ran while one was open for 4% of the time, Pallas kernels for 0%

commit v1 on v0

v1 whole, which is shorter than its diff:
```python
import math

import jax
import jax.numpy as jnp
from jax import lax
from jax.experimental import pallas as pl
from jax.experimental.pallas import tpu as pltpu
from jax.sharding import PartitionSpec as P

ITERS = 3
ACTIONS = 4
POINTS = 5
OUTS = 24
GOALS = 24
CLASSES = 16
ROWS = 16
COLS = 128
DECAY = 0.9
SLACK = 0.05
VH, RH, FH = 6, 5, 3
TOP = 16
EXT = 48
GROUP = 16
OCT = GOALS // 8
HIGHEST = lax.Precision.HIGHEST
F32 = jnp.float32
BF16 = jnp.bfloat16


def vmem_call(kernel, out_shape, scratch=(), limit=48 * 1024 * 1024):
    whole = pl.BlockSpec(memory_space=pltpu.VMEM)
    return lambda *args: pl.pallas_call(
        kernel,
        out_shape=out_shape,
        in_specs=[whole] * len(args),
        out_specs=jax.tree.map(lambda _: whole, out_shape),
        scratch_shapes=list(scratch),
        compiler_params=pltpu.CompilerParams(vmem_limit_bytes=limit),
    )(*args)


def lane_iota(shape):
    return lax.broadcasted_iota(jnp.int32, shape, len(shape) - 1)


def turn(x, shift):
    shift = shift % COLS
    return x if shift == 0 else pltpu.roll(x, shift, 1)


def dot(a, b, dims, precision=None):
    return lax.dot_general(a, b, (dims, ((), ())), precision=precision, preferred_element_type=F32)


def table_kernel(scale_ref, embed_ref, time_ref, w1_ref, w2_ref, w3_ref, tab_ref, f_ref, h1_ref, h2_ref, raw):
    scale = scale_ref[...].astype(F32) * (1.0 / 64.0)
    feature = (embed_ref[...].astype(F32) + scale * time_ref[...].astype(F32)).astype(BF16)
    one = jnp.tanh(dot(feature, w1_ref[...], ((1,), (0,)))).astype(BF16)
    two = jnp.tanh(dot(one, w2_ref[...], ((1,), (0,)))).astype(BF16)
    f_ref[...] = feature.astype(F32)
    h1_ref[...] = one.astype(F32)
    h2_ref[...] = two.astype(F32)
    logits = dot(w3_ref[...], two, ((0,), (1,)))
    raw[...] = jnp.zeros_like(raw)
    tab_ref[...] = jnp.zeros_like(tab_ref)
    for a in range(ACTIONS):
        raw[8 * a : 8 * a + POINTS, 0:CLASSES] = logits[a * POINTS : (a + 1) * POINTS]
    valid = lax.broadcasted_iota(jnp.int32, (8, COLS), 0) < POINTS
    for a in range(ACTIONS):
        x = raw[8 * a : 8 * a + 8, :]
        weight = jnp.maximum(x, 0.0) + jnp.log(1.0 + jnp.exp(-jnp.abs(x))) + SLACK
        total = jnp.sum(jnp.where(valid, weight, 0.0), axis=0, keepdims=True)
        tab_ref[16 * a : 16 * a + 8, :] = DECAY * weight / total
        tab_ref[16 * a + 8 : 16 * a + 16, :] = 1.0 / ((1.0 + jnp.exp(-x)) * total)
    tab_ref[64:68, 0:CLASSES] = logits[ACTIONS * POINTS :]


def chance_row(a, k):
    return 16 * a + k


def slope_row(a, k):
    return 16 * a + 8 + k


def bonus_row(a):
    return 64 + a


def class_plane(buf_ref, own_ref):
    up, down = buf_ref
    return up, own_ref[...].astype(F32) + 1.0, down


def fill_rows(dst, g, up, mid, down, n):
    dst[g, TOP - n : TOP, :] = up
    dst[g, TOP : TOP + ROWS, :] = mid
    dst[g, TOP + ROWS : TOP + ROWS + n, :] = down


def extend_rows(v_ref, r_ref, s_ref, c_ref, up_ref, down_ref, val, rew, sen, cls):
    def one(g, carry):
        up = up_ref[g].astype(F32)
        down = down_ref[g].astype(F32)
        fill_rows(val, g, up[0:6], v_ref[g].astype(F32), down[0:6], VH)
        fill_rows(rew, g, up[6:11], r_ref[g].astype(F32), down[6:11], RH)
        fill_rows(sen, g, up[11:14], s_ref[g].astype(F32), down[11:14], FH)
        return carry

    lax.fori_loop(0, GOALS, one, 0, unroll=4)
    cls[...] = jnp.zeros_like(cls)
    cls[TOP : TOP + ROWS, :] = c_ref[...].astype(F32) + 1.0
    for i in range(RH):
        cls[TOP - RH + i : TOP - RH + i + 1, :] = up_ref[i, 14:15, :].astype(F32)
        cls[TOP + ROWS + i : TOP + ROWS + i + 1, :] = down_ref[i, 14:15, :].astype(F32)


def strip_kernel(v_ref, r_ref, s_ref, c_ref, up_ref, down_ref, to_right, to_left, val, rew, sen, cls):
    extend_rows(v_ref, r_ref, s_ref, c_ref, up_ref, down_ref, val, rew, sen, cls)
    group_lane = lane_iota((8, COLS)) % GROUP
    group_at = lane_iota((8, COLS)) // GROUP

    def tile(i, carry):
        o, j = i // 4, i % 4
        rows = pl.ds(pl.multiple_of(8 + 8 * j, 8), 8)
        right = jnp.zeros((8, COLS), F32)
        left = jnp.zeros((8, COLS), F32)
        for q in range(8):
            p = GROUP * q
            v, r, s = val[o * 8 + q, rows, :], rew[o * 8 + q, rows, :], sen[o * 8 + q, rows, :]
            here = group_at == q
            part = jnp.where(group_lane < 6, turn(v, p + 6), jnp.where(group_lane < 11, turn(r, p + 11), turn(s, p + 14)))
            right = jnp.where(here, part, right)
            part = jnp.where(group_lane < 6, turn(v, p), jnp.where(group_lane < 11, turn(r, p + 6), turn(s, p + 11)))
            left = jnp.where(here, part, left)
        to_right[o, pl.ds(pl.multiple_of(8 * j, 8), 8), :] = right
        to_left[o, pl.ds(pl.multiple_of(8 * j, 8), 8), :] = left
        return carry

    lax.fori_loop(0, OCT * 4, tile, 0)
    for j in range(4):
        c = cls[8 + 8 * j : 16 + 8 * j, :]
        right = jnp.zeros((8, COLS), F32)
        left = jnp.zeros((8, COLS), F32)
        for q in range(8):
            here = group_at == q
            right = jnp.where(here, turn(c, GROUP * q + 6), right)
            left = jnp.where(here, turn(c, GROUP * q), left)
        to_right[OCT, 8 * j : 8 * j + 8, :] = right
        to_left[OCT, 8 * j : 8 * j + 8, :] = left


def main_kernel(v_ref, r_ref, s_ref, c_ref, up_ref, down_ref, lb_ref, rb_ref, tab_ref,
                snap_ref, pay_ref, sums_ref,
                val, rew, sen, cls, sval, srew, ssen, scls,
                chance, schance, bonus, sbonus, mask, smask, slope,
                soft, ssoft, lshift, rshift, push, spush, cgrad, paysum, packed):
    extend_rows(v_ref, r_ref, s_ref, c_ref, up_ref, down_ref, val.at[0], rew, sen, cls)
    lane = lane_iota((8, COLS))
    glane = lane % GROUP
    inner = glane < 6
    first, last = lane == 0, lane == COLS - 1
    strip_first, strip_last = glane == 5, glane == 6
    for o in range(OCT + 1):
        for j in range(4):
            left = lb_ref[o, 8 * j : 8 * j + 8, :].astype(F32)
            right = rb_ref[o, 8 * j : 8 * j + 8, :].astype(F32)
            at = slice(8 + 8 * j, 16 + 8 * j)
            outer = jnp.where(inner, left, turn(right, 6))
            if o == OCT:
                scls[at, :] = jnp.where(glane < 12, outer, 0.0)
            else:
                sval[0, o, at, :] = outer
                srew[o, at, :] = jnp.where(inner, turn(left, -5), right)
                ssen[o, at, :] = jnp.where(inner, turn(left, -8), turn(right, -5))
    for j in range(4):
        at = slice(8 + 8 * j, 16 + 8 * j)
        for source, ch, bo, ma in ((cls, chance, bonus, mask), (scls, schance, sbonus, smask)):
            number = source[at, :].astype(jnp.int32)
            inside = number > 0
            which = jnp.maximum(number - 1, 0)
            ma[at, :] = inside.astype(F32)

            def look(row):
                table = jnp.broadcast_to(tab_ref[row : row + 1, :], (8, COLS))
                return jnp.where(inside, jnp.take_along_axis(table, which, axis=1), 0.0)

            for a in range(ACTIONS):
                for k in range(POINTS):
                    ch[a * POINTS + k, at, :] = look(chance_row(a, k))
                    if source is cls and j in (1, 2):
                        slope[a * POINTS + k, 8 * j - 8 : 8 * j, :] = look(slope_row(a, k))
                bo[a, at, :] = look(bonus_row(a))

    def where_tile(j):
        base = pl.multiple_of(8 + 8 * j, 8)
        return pl.ds(base, 8), pl.ds(base - 1, 8), pl.ds(base + 1, 8)

    def soft_step(near, reward, ch, bo, keep_value):
        q = []
        for a in range(ACTIONS):
            total = reward + bo[a]
            for k in range(POINTS):
                total = total + ch[a * POINTS + k] * near[k]
            q.append(total)
        highest = jnp.maximum(jnp.maximum(q[0], q[1]), jnp.maximum(q[2], q[3]))
        e = [jnp.exp(x - highest) for x in q]
        total = (e[0] + e[1]) + (e[2] + e[3])
        inverse = 1.0 / total
        value = highest + jnp.log(total) if keep_value else None
        return [x * inverse for x in e], value

    for t in range(ITERS):
        keep = t < ITERS - 1

        def forward(i, carry, t=t, keep=keep):
            o, j = i // 4, i % 4
            rows, above, below = where_tile(j)
            ch = [chance[n, rows, :] for n in range(ACTIONS * POINTS)]
            bo = [bonus[a, rows, :] for a in range(ACTIONS)]
            sv = sval[t, o, rows, :]
            edge = jnp.zeros((8, COLS), F32)
            for q in range(8):
                p, g = GROUP * q, o * 8 + q
                x = val[t, g, rows, :]
                fill = turn(sv, -(p + 6))
                toleft = turn(jnp.where(last, fill, x), 1)
                toright = turn(jnp.where(first, fill, x), -1)
                edge = jnp.where((lane == p + 5) | (lane == p + 6), turn(x, p + 6), edge)
                lshift[t, g, rows, :] = toleft
                rshift[t, g, rows, :] = toright
                near = [x, val[t, g, above, :], val[t, g, below, :], toleft, toright]
                probs, value = soft_step(near, rew[g, rows, :], ch, bo, keep)
                for a in range(ACTIONS):
                    soft[t, a, g, rows, :] = probs[a]
                if keep:
                    val[t + 1, g, rows, :] = value * mask[rows, :]
            near = [sv, sval[t, o, above, :], sval[t, o, below, :],
                    turn(jnp.where(strip_first, edge, sv), 1), turn(jnp.where(strip_last, edge, sv), -1)]
            ch = [schance[n, rows, :] for n in range(ACTIONS * POINTS)]
            bo = [sbonus[a, rows, :] for a in range(ACTIONS)]
            probs, value = soft_step(near, srew[o, rows, :], ch, bo, keep)
            for a in range(ACTIONS):
                ssoft[t, a, o, rows, :] = probs[a]
            if keep:
                sval[t + 1, o, rows, :] = value * smask[rows, :]
            return carry

        lax.fori_loop(0, OCT * 4, forward, 0)

    cgrad[...] = jnp.zeros_like(cgrad)
    paysum[...] = jnp.zeros_like(paysum)

    def gather(o, rows, above, below, old):
        s3, s4 = spush[old, 3, o, rows, :], spush[old, 4, o, rows, :]
        both = jnp.where(strip_last, s3, s4)
        edge = jnp.zeros((8, COLS), F32)
        out = []
        for q in range(8):
            p, g = GROUP * q, o * 8 + q
            p3, p4 = push[old, 3, g, rows, :], push[old, 4, g, rows, :]
            fill = turn(both, -(p + 6))
            from_right = turn(jnp.where(first, fill, p3), -1)
            from_left = turn(jnp.where(last, fill, p4), 1)
            edge = jnp.where((lane == p + 5) | (lane == p + 6), turn(jnp.where(first, p3, p4), p + 6), edge)
            out.append(push[old, 0, g, rows, :] + push[old, 1, g, below, :] + push[old, 2, g, above, :]
                       + from_right + from_left)
        strip = (spush[old, 0, o, rows, :] + spush[old, 1, o, below, :] + spush[old, 2, o, above, :]
                 + turn(jnp.where(strip_last, edge, s3), -1) + turn(jnp.where(strip_first, edge, s4), 1))
        return out, strip

    for t in reversed(range(ITERS)):
        new, old = t % 2, (t + 1) % 2

        def backward(o, j, own, t=t, new=new, old=old):
            rows, above, below = where_tile(j)
            if t == ITERS - 1:
                adj = [sen[o * 8 + q, rows, :] for q in range(8)]
                strip = ssen[o, rows, :]
            else:
                adj, strip = gather(o, rows, above, below, old)
            for q in range(8):
                g = o * 8 + q
                grads = [adj[q] * soft[t, a, g, rows, :] for a in range(ACTIONS)]
                for k in range(POINTS):
                    total = grads[0] * chance[k, rows, :]
                    for a in range(1, ACTIONS):
                        total = total + grads[a] * chance[a * POINTS + k, rows, :]
                    push[new, k, g, rows, :] = total
                if own:
                    at = pl.ds(pl.multiple_of(8 * j - 8, 8), 8)
                    paysum[g, at, :] += (grads[0] + grads[1]) + (grads[2] + grads[3])
                    near = [val[t, g, rows, :], val[t, g, above, :], val[t, g, below, :],
                            lshift[t, g, rows, :], rshift[t, g, rows, :]]
                    for a in range(ACTIONS):
                        for k in range(POINTS):
                            cgrad[a * POINTS + k, at, :] += grads[a] * near[k]
                        cgrad[ACTIONS * POINTS + a, at, :] += grads[a]
            grads = [strip * ssoft[t, a, o, rows, :] for a in range(ACTIONS)]
            for k in range(POINTS):
                total = grads[0] * schance[k, rows, :]
                for a in range(1, ACTIONS):
                    total = total + grads[a] * schance[a * POINTS + k, rows, :]
                spush[new, k, o, rows, :] = total

        def outer_rows(i, carry):
            backward(i // 2, 3 * (i % 2), False)
            return carry

        def own_rows(i, carry):
            backward(i // 2, 1 + i % 2, True)
            return carry

        lax.fori_loop(0, OCT * 2, outer_rows, 0)
        lax.fori_loop(0, OCT * 2, own_rows, 0)

    def finish(i, carry):
        o, j = i // 2, 1 + i % 2
        rows, above, below = where_tile(j)
        adj = gather(o, rows, above, below, 0)[0]
        at = pl.ds(pl.multiple_of(8 * j - 8, 8), 8)
        for q in range(8):
            packed[o * 8 + q, at, :] = adj[q]
        return carry

    lax.fori_loop(0, OCT * 2, finish, 0)
    snap_ref[...] = packed[...].astype(BF16)
    pay_ref[...] = paysum[...].astype(BF16)
    for j in range(2):
        at = slice(8 * j, 8 * j + 8)
        rows = slice(TOP + 8 * j, TOP + 8 * j + 8)
        for a in range(ACTIONS):
            grads = [cgrad[a * POINTS + k, at, :] for k in range(POINTS)]
            weighted = grads[0] * chance[a * POINTS, rows, :]
            for k in range(1, POINTS):
                weighted = weighted + grads[k] * chance[a * POINTS + k, rows, :]
            for k in range(POINTS):
                cgrad[a * POINTS + k, at, :] = (DECAY * grads[k] - weighted) * slope[a * POINTS + k, at, :]
    number = lax.broadcasted_iota(jnp.int32, (CLASSES, COLS), 0)
    total = jnp.zeros((CLASSES, OUTS), F32)
    for i in range(ROWS):
        one_hot = (number == c_ref[i : i + 1, :]).astype(BF16)
        total = total + dot(one_hot, cgrad[:, i, :].astype(BF16), ((1,), (1,)))
    packed[0, :, :] = jnp.zeros((ROWS, COLS), F32)
    packed[0, 0:CLASSES, 0:OUTS] = total
    sums_ref[...] = packed[0, 0:8, :] + turn(packed[0, 8:16, :], 32)


def last_kernel(parts_ref, scale_ref, f_ref, h1_ref, h2_ref, w1_ref, w2_ref, w3_ref,
                embed_ref, time_ref, one_ref, two_ref, three_ref, *, factor):
    total = parts_ref[0]
    for i in range(1, parts_ref.shape[0]):
        total = total + parts_ref[i]
    total = total * factor
    sums = jnp.concatenate([total[:, 0:OUTS], turn(total, -32)[:, 0:OUTS]], axis=0)
    f, h1, h2 = f_ref[...], h1_ref[...], h2_ref[...]
    two_grad = dot(sums, w3_ref[...].astype(F32), ((1,), (1,)), HIGHEST) * (1.0 - h2 * h2)
    one_grad = dot(two_grad, w2_ref[...].astype(F32), ((1,), (1,)), HIGHEST) * (1.0 - h1 * h1)
    feature_grad = dot(one_grad, w1_ref[...].astype(F32), ((1,), (1,)), HIGHEST)
    three_ref[...] = dot(h2, sums, ((0,), (0,)), HIGHEST)
    two_ref[...] = dot(h1, two_grad, ((0,), (0,)), HIGHEST)
    one_ref[...] = dot(f, one_grad, ((0,), (0,)), HIGHEST)
    embed_ref[...] = feature_grad
    scale = scale_ref[...].astype(F32) * (1.0 / 64.0)
    time_ref[...] = scale * jnp.sum(feature_grad, axis=0, keepdims=True)


def shift(x, axis, step):
    size = lax.axis_size(axis)
    pairs = [(i, i + step) for i in range(size) if 0 <= i + step < size]
    return lax.ppermute(x, axis, pairs)


def spread(x, axis):
    size = lax.axis_size(axis)
    return lax.all_to_all(jnp.broadcast_to(x[None], (size,) + x.shape), axis, 0, 0, tiled=True)


def body(classes, check_index, snapshot, payoff, sensitivity, embed, time_vec, w_one, w_two, w_three):
    sd = jax.ShapeDtypeStruct
    marked = (classes + 1).astype(BF16)

    def edge_rows(v, r, s, c):
        c = jnp.pad(c[:, None, :], ((0, GOALS - RH), (0, 1), (0, 0)))
        return jnp.concatenate([v, r, s, c], axis=1)

    to_down = edge_rows(snapshot[:, -VH:], payoff[:, -RH:], sensitivity[:, -FH:], marked[-RH:])
    to_up = edge_rows(snapshot[:, :VH], payoff[:, :RH], sensitivity[:, :FH], marked[:RH])
    up = shift(to_down, "row", 1)
    down = shift(to_up, "row", -1)

    scale = jnp.broadcast_to(check_index.reshape(1, 1), (1, 64))
    layer = sd((CLASSES, 64), F32)
    table, feature, one, two = vmem_call(
        table_kernel, (sd((72, COLS), F32), layer, layer, layer), [pltpu.VMEM((32, COLS), F32)]
    )(scale, embed, time_vec.reshape(1, -1), w_one, w_two, w_three)

    ext = pltpu.VMEM((GOALS, EXT, COLS), F32)
    plane = pltpu.VMEM((EXT, COLS), F32)
    edge = sd((OCT + 1, 32, COLS), F32)
    to_right, to_left = vmem_call(strip_kernel, (edge, edge), [ext, ext, ext, plane])(
        snapshot, payoff, sensitivity, classes, up, down
    )
    left = shift(to_right.astype(BF16), "col", 1)
    right = shift(to_left.astype(BF16), "col", -1)

    tile = sd((GOALS, ROWS, COLS), BF16)
    strip = pltpu.VMEM((OCT, EXT, COLS), F32)

    def many(*shape):
        return pltpu.VMEM(shape + (COLS,), F32)

    n = ACTIONS * POINTS
    snap, pay, sums = vmem_call(
        main_kernel,
        (tile, tile, sd((8, COLS), F32)),
        [
            many(ITERS, GOALS, EXT), ext, ext, plane,
            many(ITERS, OCT, EXT), strip, strip, plane,
            many(n, EXT), many(n, EXT), many(ACTIONS, EXT), many(ACTIONS, EXT), plane, plane, many(n, ROWS),
            many(ITERS, ACTIONS, GOALS, EXT), many(ITERS, ACTIONS, OCT, EXT),
            many(ITERS, GOALS, EXT), many(ITERS, GOALS, EXT),
            many(2, POINTS, GOALS, EXT), many(2, POINTS, OCT, EXT),
            many(OUTS, ROWS), many(GOALS, ROWS), many(GOALS, ROWS),
        ],
    )(snapshot, payoff, sensitivity, classes, up, down, left, right, table)

    sums = jnp.sum(spread(sums, "row"), axis=0)
    parts = spread(sums, "col")
    factor = 1.0 / math.sqrt(ROWS * lax.axis_size("row") * COLS * lax.axis_size("col"))

    def last(*refs):
        last_kernel(*refs, factor=factor)

    grads = vmem_call(
        last, (layer, sd((1, 64), F32), sd((64, 64), F32), sd((64, 64), F32), sd((64, OUTS), F32))
    )(parts, scale, feature, one, two, w_one, w_two, w_three)
    return (snap, pay, grads[0], grads[1].reshape(64), grads[2], grads[3], grads[4])


def solution(mesh):
    tiled = P(None, "row", "col")
    return jax.shard_map(
        body,
        mesh=mesh,
        in_specs=(P("row", "col"), P(), tiled, tiled, tiled, P(), P(), P(), P(), P()),
        out_specs=(tiled, tiled, P(), P(), P(), P(), P()),
        check_vma=False,
    )
```

time: 264 us -> 97.3 us (0.37); the launches traced: 260 us -> 96.9 us
  blocking collectives: 117 us -> 46 us
  starting transfers between devices: 63.6 us -> 14.4 us
  waiting for transfers between devices: 33.3 us -> 4.07 us
  Pallas kernels: 0 us -> 26.7 us
  other arithmetic: 21.6 us -> 0.9 us
  local copies, waits for them, and re-layouts: 18.9 us -> 3.25 us
    psum x1 -> x0, blocking collectives: 117 us -> none  [body(): lax.psum((gradients[0], gradients[1], gradients[2], gradients[3], gradien...]
    ppermute x24 -> x4, starting transfers between devices: 63.6 us -> 14.4 us  [shift(): return lax.ppermute(x, axis, pairs)]
    all_to_all x0 -> x2, blocking collectives: none -> 46 us  [spread(): lax.all_to_all(jnp.broadcast_to(x[None], (size,) + x.shape), axis, 0, 0,...]
    ppermute x24 -> x4, waiting for transfers between devices: 33.3 us -> 4.07 us  [shift(): return lax.ppermute(x, axis, pairs)]
    pallas_call x0 -> x4, Pallas kernels: none -> 26.7 us  [vmem_call(): pl.pallas_call(kernel, out_shape=out_shape, in_specs=[whole] * len(args),...]
    scatter-add x12 -> x0, local copies, waits for them, and re-layouts: 8.44 us -> none  [the longest x6 7.97 us: body(): worth_sensitivity = worth_sensitivity.at[:, :, 0].add(from_cols[:, :, 0])...]
    add x18 -> x0, other arithmetic: 7.66 us -> none  [the longest x6 4.56 us: body(): worth_sensitivity = worth_sensitivity.at[:, :, 0].add(from_cols[:, :, 0])...]
    reduce_sum x8 -> x1, other arithmetic: 6.9 us -> 0.02 us  [body(): sums = jnp.sum(spread(sums, 'row'), axis=0)]
  transfers between devices with their start and end apart: 24 -> 4, of which waited for: 11 -> 2; matrix products, arithmetic and copies ran while one was open for 4% -> 0% of each run, Pallas kernels for 0% -> 0%
where the time goes in v1:
time: 97.3 us; the launch traced here: 96.9 us
  blocking collectives  46 us (47%)
  Pallas kernels  26.7 us (27%)
  starting transfers between devices  14.4 us (15%)
  waiting for transfers between devices  4.07 us (4%)
  local copies, waits for them, and re-layouts  3.25 us (3%)
  between operations  1.51 us (2%)
    all_to_all x2, blocking collectives, spread(): lax.all_to_all(jnp.broadcast_to(x[None], (size,) + x.shape), axis, 0, 0,...  46 us
    pallas_call x4, Pallas kernels, vmem_call(): pl.pallas_call(kernel, out_shape=out_shape, in_specs=[whole] * len(args),...  26.7 us
    ppermute x4, starting transfers between devices, shift(): return lax.ppermute(x, axis, pairs)  14.4 us
    ppermute x4, waiting for transfers between devices, shift(): return lax.ppermute(x, axis, pairs)  4.07 us
    unnamed x20, local copies, waits for them, and re-layouts  2.31 us
  transfers between devices with their start and end apart: 4, of which 2 were waited for; matrix products, arithmetic and copies ran while one was open for 0% of the time, Pallas kernels for 0%

profile of v1, /device:TPU:1, one launch (start us, length us, event | category | flops | bytes accessed | tf_op | source)
XLA Modules:
  0.0 96.9 jit_solution(16572550087802139778)
XLA Ops:
  0.6 0.7 add_convert_fusion
  1.4 0.8 fusion.6
  2.3 0.0 copy-start.1
  2.3 0.9 copy-done.1
  3.2 0.1 fusion.2
  3.2 4.0 %collective-permute-start = (bf16[24,16,128]{2,1,0:T(8,128)(2,1)S(1)}, bf16[24,16,128]{2,1,0:T(8,128)(2,1)S(1)}, u32[]{:S(2)}, u32[]{:S(2)}) collective-permute-start(bf16[24,16,128]{2,1,0:T(8,128)(2,1)S(1)} %fusion.2), channel_id=1, source_target_pairs={{0,32},{32,64},{64,96},{96,128},{128,160},{160,192},{192,224},{224... | collective-permute-start | bytes 294920 | tf_op jit(solution)/shard_map/ppermute | solution.py:371
  7.3 0.0 copy-start.3
  7.3 0.1 fusion.3
  7.4 1.3 %collective-permute-start.1 = (bf16[24,16,128]{2,1,0:T(8,128)(2,1)S(1)}, bf16[24,16,128]{2,1,0:T(8,128)(2,1)S(1)}, u32[]{:S(2)}, u32[]{:S(2)}) collective-permute-start(bf16[24,16,128]{2,1,0:T(8,128)(2,1)S(1)} %fusion.3), channel_id=1, source_target_pairs={{32,0},{64,32},{96,64},{128,96},{160,128},{192,160},{224,192},{256... | collective-permute-start | bytes 294920 | tf_op jit(solution)/shard_map/ppermute | solution.py:371
  8.7 0.2 collective-permute-done.up_ref
  8.9 3.9 %collective-permute-done.1.down_ref = bf16[24,16,128]{2,1,0:T(8,128)(2,1)S(1)} collective-permute-done((bf16[24,16,128]{2,1,0:T(8,128)(2,1)S(1)}, bf16[24,16,128]{2,1,0:T(8,128)(2,1)S(1)}, u32[]{:S(2)}, u32[]{:S(2)}) %collective-permute-start.1) | collective-permute-done | bytes 98336 | tf_op jit(solution)/shard_map/ppermute | solution.py:371
  12.8 1.7 %shard_map.153 = (f32[4,32,128]{2,1,0:T(8,128)S(1)}, f32[4,32,128]{2,1,0:T(8,128)S(1)}) custom-call(bf16[24,16,128]{2,1,0:T(8,128)(2,1)S(1)} %copy-done, bf16[24,16,128]{2,1,0:T(8,128)(2,1)S(1)} %copy-done.1, bf16[24,16,128]{2,1,0:T(8,128)(2,1)S(1)} %copy-done.2, s32[16,128]{1,0:T(8,128)S(1)} %copy-done.3, ...), custom_call_target="tpu_custom_call" | custom-call | tf_op jit(solution)/shard_map/pallas_call | solution.py:32
  14.4 0.0 copy-start.8
  14.5 0.0 copy-start.4
  14.5 7.2 %collective-permute-start.3 = (bf16[4,32,128]{2,1,0:T(8,128)(2,1)S(1)}, bf16[4,32,128]{2,1,0:T(8,128)(2,1)S(1)}, u32[]{:S(2)}, u32[]{:S(2)}) collective-permute-start(bf16[4,32,128]{2,1,0:T(8,128)(2,1)S(1)} %convert_element_type.14), channel_id=1, source_target_pairs={{1,0},{2,1},{3,2},{4,3},{5,4},{6,5},{7,6},{8,7},{9,8},{10,9},{11,1... | collective-permute-start | bytes 98312 | tf_op jit(solution)/shard_map/ppermute | solution.py:371
  21.7 1.9 %collective-permute-start.2 = (bf16[4,32,128]{2,1,0:T(8,128)(2,1)S(1)}, bf16[4,32,128]{2,1,0:T(8,128)(2,1)S(1)}, u32[]{:S(2)}, u32[]{:S(2)}) collective-permute-start(bf16[4,32,128]{2,1,0:T(8,128)(2,1)S(1)} %convert_element_type.13), channel_id=1, source_target_pairs={{0,1},{1,2},{2,3},{3,4},{4,5},{5,6},{6,7},{7,8},{8,9},{9,10},{10,1... | collective-permute-start | bytes 98312 | tf_op jit(solution)/shard_map/ppermute | solution.py:371
  24.3 0.1 copy.32.w3_ref.refs_7_
  24.4 0.6 copy-done.6
  25.1 0.4 shard_map.154
  25.5 23.2 %shard_map.155 = (bf16[24,16,128]{2,1,0:T(8,128)(2,1)}, bf16[24,16,128]{2,1,0:T(8,128)(2,1)}, f32[8,128]{1,0:T(8,128)S(1)}) custom-call(bf16[24,16,128]{2,1,0:T(8,128)(2,1)S(1)} %copy-done, bf16[24,16,128]{2,1,0:T(8,128)(2,1)S(1)} %copy-done.1, bf16[24,16,128]{2,1,0:T(8,128)(2,1)S(1)} %copy-done.2, s32[16,128]{1,0:T(8,128)S(1)} %copy-done.3, ...), custom_call_target="tpu_custom_call" | custom-call | tf_op jit(solution)/shard_map/pallas_call | solution.py:32
  48.8 12.7 %all_to_all.10 = f32[16,8,128]{2,1,0:T(8,128)S(1)} all-to-all(f32[16,8,128]{2,1,0:T(8,128)S(1)} %broadcast_in_dim.29), channel_id=1, replica_groups=mesh['row'=16,'col'=32] {'row'}, dimensions={0} | all-to-all | bytes 131072 | tf_op jit(solution)/shard_map/all_to_all | solution.py:376
  61.5 33.4 %all_to_all.11.refs_0_ = f32[32,8,128]{2,1,0:T(8,128)S(1)} all-to-all(f32[32,8,128]{2,1,0:T(8,128)S(1)} %broadcast_in_dim.30), channel_id=1, replica_groups=mesh['row'=16,'col'=32] {'col'}, dimensions={0} | all-to-all | bytes 262144 | tf_op jit(solution)/shard_map/all_to_all | solution.py:376
  94.8 1.4 %shard_map.156 = (f32[16,64]{1,0:T(8,128)}, f32[1,64]{1,0:T(1,128)}, f32[64,64]{1,0:T(8,128)}, f32[64,64]{1,0:T(8,128)}, f32[64,24]{1,0:T(8,128)S(1)}) custom-call(f32[32,8,128]{2,1,0:T(8,128)S(1)} %all_to_all.11.refs_0_, s32[1,64]{1,0:T(1,128)S(1)} %broadcast_in_dim.28.scale_ref.refs_1_, f32[16,64]{1,0:T(8,128)S(1)} %get-tuple-element.27.refs_2_, ...), custom_call_target="tpu_custom_call" | custom-call | tf_op jit(solution)/shard_map/pallas_call | solution.py:32
  96.2 0.7 copy.34
  (25 shorter events, 0.2 us)
Async XLA Ops:
  0.6 1.6 %copy-start = (bf16[24,16,128]{2,1,0:T(8,128)(2,1)S(1)}, bf16[24,16,128]{2,1,0:T(8,128)(2,1)}, u32[]{:S(2)}) copy-start(bf16[24,16,128]{2,1,0:T(8,128)(2,1)} %v_ref.3) | copy-start | bytes 294916
  2.3 0.9 copy-start.1
  3.2 5.7 %collective-permute-start = (bf16[24,16,128]{2,1,0:T(8,128)(2,1)S(1)}, bf16[24,16,128]{2,1,0:T(8,128)(2,1)S(1)}, u32[]{:S(2)}, u32[]{:S(2)}) collective-permute-start(bf16[24,16,128]{2,1,0:T(8,128)(2,1)S(1)} %fusion.2), channel_id=1, source_target_pairs={{0,32},{32,64},{64,96},{96,128},{128,160},{160,192},{192,224},{224... | collective-permute-start | bytes 294920 | tf_op jit(solution)/shard_map/ppermute | solution.py:371
  7.3 5.5 %copy-start.2 = (bf16[24,16,128]{2,1,0:T(8,128)(2,1)S(1)}, bf16[24,16,128]{2,1,0:T(8,128)(2,1)}, u32[]{:S(2)}) copy-start(bf16[24,16,128]{2,1,0:T(8,128)(2,1)} %s_ref.3) | copy-start | bytes 294916
  7.3 5.5 %copy-start.3 = (s32[16,128]{1,0:T(8,128)S(1)}, s32[16,128]{1,0:T(8,128)}, u32[]{:S(2)}) copy-start(s32[16,128]{1,0:T(8,128)} %c_ref.3) | copy-start | bytes 24580
  7.4 5.4 %collective-permute-start.1 = (bf16[24,16,128]{2,1,0:T(8,128)(2,1)S(1)}, bf16[24,16,128]{2,1,0:T(8,128)(2,1)S(1)}, u32[]{:S(2)}, u32[]{:S(2)}) collective-permute-start(bf16[24,16,128]{2,1,0:T(8,128)(2,1)S(1)} %fusion.3), channel_id=1, source_target_pairs={{32,0},{64,32},{96,64},{128,96},{160,128},{192,160},{224,192},{256... | collective-permute-start | bytes 294920 | tf_op jit(solution)/shard_map/ppermute | solution.py:371
  14.4 9.8 %copy-start.8 = (bf16[64,24]{0,1:T(8,128)(2,1)S(1)}, bf16[64,24]{0,1:T(8,128)(2,1)}, u32[]{:S(2)}) copy-start(bf16[64,24]{0,1:T(8,128)(2,1)} %param.19) | copy-start | bytes 9220
  14.5 10.0 %copy-start.5 = (bf16[64,64]{1,0:T(8,128)(2,1)S(1)}, bf16[64,64]{1,0:T(8,128)(2,1)}, u32[]{:S(2)}) copy-start(bf16[64,64]{1,0:T(8,128)(2,1)} %refs_6_.1) | copy-start | bytes 24580
  14.5 9.9 %copy-start.4 = (bf16[64,64]{1,0:T(8,128)(2,1)S(1)}, bf16[64,64]{1,0:T(8,128)(2,1)}, u32[]{:S(2)}) copy-start(bf16[64,64]{1,0:T(8,128)(2,1)} %refs_5_.1) | copy-start | bytes 24580
  14.5 11.0 %collective-permute-start.3 = (bf16[4,32,128]{2,1,0:T(8,128)(2,1)S(1)}, bf16[4,32,128]{2,1,0:T(8,128)(2,1)S(1)}, u32[]{:S(2)}, u32[]{:S(2)}) collective-permute-start(bf16[4,32,128]{2,1,0:T(8,128)(2,1)S(1)} %convert_element_type.14), channel_id=1, source_target_pairs={{1,0},{2,1},{3,2},{4,3},{5,4},{6,5},{7,6},{8,7},{9,8},{10,9},{11,1... | collective-permute-start | bytes 98312 | tf_op jit(solution)/shard_map/ppermute | solution.py:371
  21.7 3.8 %collective-permute-start.2 = (bf16[4,32,128]{2,1,0:T(8,128)(2,1)S(1)}, bf16[4,32,128]{2,1,0:T(8,128)(2,1)S(1)}, u32[]{:S(2)}, u32[]{:S(2)}) collective-permute-start(bf16[4,32,128]{2,1,0:T(8,128)(2,1)S(1)} %convert_element_type.13), channel_id=1, source_target_pairs={{0,1},{1,2},{2,3},{3,4},{4,5},{5,6},{6,7},{7,8},{8,9},{9,10},{10,1... | collective-permute-start | bytes 98312 | tf_op jit(solution)/shard_map/ppermute | solution.py:371
  24.4 0.7 copy-start.6
  24.4 0.7 copy-start.7

commit v2 on v1

--- a/solution.py
+++ b/solution.py
@@ -27,12 +27,13 @@
 BF16 = jnp.bfloat16
 
 
-def vmem_call(kernel, out_shape, scratch=(), limit=48 * 1024 * 1024):
+def vmem_call(kernel, out_shape, scratch=(), limit=48 * 1024 * 1024, source=pltpu.VMEM):
     whole = pl.BlockSpec(memory_space=pltpu.VMEM)
+    given = pl.BlockSpec(memory_space=source)
     return lambda *args: pl.pallas_call(
         kernel,
         out_shape=out_shape,
-        in_specs=[whole] * len(args),
+        in_specs=[given] * len(args),
         out_specs=jax.tree.map(lambda _: whole, out_shape),
         scratch_shapes=list(scratch),
         compiler_params=pltpu.CompilerParams(vmem_limit_bytes=limit),
@@ -60,7 +61,7 @@
     f_ref[...] = feature.astype(F32)
     h1_ref[...] = one.astype(F32)
     h2_ref[...] = two.astype(F32)
-    logits = dot(w3_ref[...], two, ((0,), (1,)))
+    logits = dot(w3_ref[...], two, ((1,), (1,)))
     raw[...] = jnp.zeros_like(raw)
     tab_ref[...] = jnp.zeros_like(tab_ref)
     for a in range(ACTIONS):
@@ -87,9 +88,24 @@
     return 64 + a
 
 
-def class_plane(buf_ref, own_ref):
-    up, down = buf_ref
-    return up, own_ref[...].astype(F32) + 1.0, down
+def edge_kernel(v_hbm, r_hbm, s_hbm, c_hbm, to_down, to_up, low, high, v_ref, r_ref, s_ref, c_ref, sems):
+    pairs = ((v_hbm, v_ref), (r_hbm, r_ref), (s_hbm, s_ref), (c_hbm, c_ref))
+    copies = [pltpu.make_async_copy(a, b, sems.at[i]) for i, (a, b) in enumerate(pairs)]
+    for copy in copies:
+        copy.start()
+    for copy in copies:
+        copy.wait()
+    low[...] = jnp.zeros_like(low)
+    high[...] = jnp.zeros_like(high)
+    marked = c_ref[...].astype(F32) + 1.0
+    for g in range(GOALS):
+        v, r, s = v_ref[g].astype(F32), r_ref[g].astype(F32), s_ref[g].astype(F32)
+        low[0:6, :], low[6:11, :], low[11:14, :] = v[ROWS - VH :], r[ROWS - RH :], s[ROWS - FH :]
+        high[0:6, :], high[6:11, :], high[11:14, :] = v[0:VH], r[0:RH], s[0:FH]
+        if g < RH:
+            low[14:15, :], high[14:15, :] = marked[ROWS - RH + g : ROWS - RH + g + 1], marked[g : g + 1]
+        to_down[g] = low[...].astype(BF16)
+        to_up[g] = high[...].astype(BF16)
 
 
 def fill_rows(dst, g, up, mid, down, n):
@@ -120,24 +136,24 @@
     group_lane = lane_iota((8, COLS)) % GROUP
     group_at = lane_iota((8, COLS)) // GROUP
 
-    def tile(i, carry):
-        o, j = i // 4, i % 4
-        rows = pl.ds(pl.multiple_of(8 + 8 * j, 8), 8)
-        right = jnp.zeros((8, COLS), F32)
-        left = jnp.zeros((8, COLS), F32)
-        for q in range(8):
-            p = GROUP * q
-            v, r, s = val[o * 8 + q, rows, :], rew[o * 8 + q, rows, :], sen[o * 8 + q, rows, :]
-            here = group_at == q
-            part = jnp.where(group_lane < 6, turn(v, p + 6), jnp.where(group_lane < 11, turn(r, p + 11), turn(s, p + 14)))
-            right = jnp.where(here, part, right)
-            part = jnp.where(group_lane < 6, turn(v, p), jnp.where(group_lane < 11, turn(r, p + 6), turn(s, p + 11)))
-            left = jnp.where(here, part, left)
-        to_right[o, pl.ds(pl.multiple_of(8 * j, 8), 8), :] = right
-        to_left[o, pl.ds(pl.multiple_of(8 * j, 8), 8), :] = left
+    def octet(o, carry):
+        for j in range(4):
+            rows = slice(8 + 8 * j, 16 + 8 * j)
+            right = jnp.zeros((8, COLS), F32)
+            left = jnp.zeros((8, COLS), F32)
+            for q in range(8):
+                p = GROUP * q
+                v, r, s = val[o * 8 + q, rows, :], rew[o * 8 + q, rows, :], sen[o * 8 + q, rows, :]
+                here = group_at == q
+                part = jnp.where(group_lane < 11, turn(r, p + 11), turn(s, p + 14))
+                right = jnp.where(here, jnp.where(group_lane < 6, turn(v, p + 6), part), right)
+                part = jnp.where(group_lane < 11, turn(r, p + 6), turn(s, p + 11))
+                left = jnp.where(here, jnp.where(group_lane < 6, turn(v, p), part), left)
+            to_right[o, 8 * j : 8 * j + 8, :] = right.astype(to_right.dtype)
+            to_left[o, 8 * j : 8 * j + 8, :] = left.astype(to_left.dtype)
         return carry
 
-    lax.fori_loop(0, OCT * 4, tile, 0)
+    lax.fori_loop(0, OCT, octet, 0)
     for j in range(4):
         c = cls[8 + 8 * j : 16 + 8 * j, :]
         right = jnp.zeros((8, COLS), F32)
@@ -146,8 +162,8 @@
             here = group_at == q
             right = jnp.where(here, turn(c, GROUP * q + 6), right)
             left = jnp.where(here, turn(c, GROUP * q), left)
-        to_right[OCT, 8 * j : 8 * j + 8, :] = right
-        to_left[OCT, 8 * j : 8 * j + 8, :] = left
+        to_right[OCT, 8 * j : 8 * j + 8, :] = right.astype(to_right.dtype)
+        to_left[OCT, 8 * j : 8 * j + 8, :] = left.astype(to_left.dtype)
 
 
 def main_kernel(v_ref, r_ref, s_ref, c_ref, up_ref, down_ref, lb_ref, rb_ref, tab_ref,
@@ -193,8 +209,8 @@
                 bo[a, at, :] = look(bonus_row(a))
 
     def where_tile(j):
-        base = pl.multiple_of(8 + 8 * j, 8)
-        return pl.ds(base, 8), pl.ds(base - 1, 8), pl.ds(base + 1, 8)
+        base = 8 + 8 * j
+        return slice(base, base + 8), slice(base - 1, base + 7), slice(base + 1, base + 9)
 
     def soft_step(near, reward, ch, bo, keep_value):
         q = []
@@ -213,8 +229,7 @@
     for t in range(ITERS):
         keep = t < ITERS - 1
 
-        def forward(i, carry, t=t, keep=keep):
-            o, j = i // 4, i % 4
+        def forward(o, j, t=t, keep=keep):
             rows, above, below = where_tile(j)
             ch = [chance[n, rows, :] for n in range(ACTIONS * POINTS)]
             bo = [bonus[a, rows, :] for a in range(ACTIONS)]
@@ -244,9 +259,13 @@
                 ssoft[t, a, o, rows, :] = probs[a]
             if keep:
                 sval[t + 1, o, rows, :] = value * smask[rows, :]
+
+        def forward_all(o, carry, forward=forward):
+            for j in range(4):
+                forward(o, j)
             return carry
 
-        lax.fori_loop(0, OCT * 4, forward, 0)
+        lax.fori_loop(0, OCT, forward_all, 0)
 
     cgrad[...] = jnp.zeros_like(cgrad)
     paysum[...] = jnp.zeros_like(paysum)
@@ -287,15 +306,25 @@
                     for a in range(1, ACTIONS):
                         total = total + grads[a] * chance[a * POINTS + k, rows, :]
                     push[new, k, g, rows, :] = total
-                if own:
-                    at = pl.ds(pl.multiple_of(8 * j - 8, 8), 8)
+            if own:
+                at = slice(8 * j - 8, 8 * j)
+                for q in range(8):
+                    g = o * 8 + q
+                    grads = [adj[q] * soft[t, a, g, rows, :] for a in range(ACTIONS)]
                     paysum[g, at, :] += (grads[0] + grads[1]) + (grads[2] + grads[3])
-                    near = [val[t, g, rows, :], val[t, g, above, :], val[t, g, below, :],
-                            lshift[t, g, rows, :], rshift[t, g, rows, :]]
-                    for a in range(ACTIONS):
-                        for k in range(POINTS):
-                            cgrad[a * POINTS + k, at, :] += grads[a] * near[k]
-                        cgrad[ACTIONS * POINTS + a, at, :] += grads[a]
+                for a in range(ACTIONS):
+                    sums = [cgrad[a * POINTS + k, at, :] for k in range(POINTS)]
+                    total = cgrad[ACTIONS * POINTS + a, at, :]
+                    for q in range(8):
+                        g = o * 8 + q
+                        grad = adj[q] * soft[t, a, g, rows, :]
+                        total = total + grad
+                        near = [val[t, g, rows, :], val[t, g, above, :], val[t, g, below, :],
+                                lshift[t, g, rows, :], rshift[t, g, rows, :]]
+                        sums = [x + grad * y for x, y in zip(sums, near)]
+                    for k in range(POINTS):
+                        cgrad[a * POINTS + k, at, :] = sums[k]
+                    cgrad[ACTIONS * POINTS + a, at, :] = total
             grads = [strip * ssoft[t, a, o, rows, :] for a in range(ACTIONS)]
             for k in range(POINTS):
                 total = grads[0] * schance[k, rows, :]
@@ -303,27 +332,22 @@
                     total = total + grads[a] * schance[a * POINTS + k, rows, :]
                 spush[new, k, o, rows, :] = total
 
-        def outer_rows(i, carry):
-            backward(i // 2, 3 * (i % 2), False)
+        def backward_all(o, carry, backward=backward):
+            for j in range(4):
+                backward(o, j, j in (1, 2))
             return carry
 
-        def own_rows(i, carry):
-            backward(i // 2, 1 + i % 2, True)
-            return carry
-
-        lax.fori_loop(0, OCT * 2, outer_rows, 0)
-        lax.fori_loop(0, OCT * 2, own_rows, 0)
-
-    def finish(i, carry):
-        o, j = i // 2, 1 + i % 2
-        rows, above, below = where_tile(j)
-        adj = gather(o, rows, above, below, 0)[0]
-        at = pl.ds(pl.multiple_of(8 * j - 8, 8), 8)
-        for q in range(8):
-            packed[o * 8 + q, at, :] = adj[q]
+        lax.fori_loop(0, OCT, backward_all, 0)
+
+    def finish(o, carry):
+        for j in (1, 2):
+            rows, above, below = where_tile(j)
+            adj = gather(o, rows, above, below, 0)[0]
+            for q in range(8):
+                packed[o * 8 + q, 8 * j - 8 : 8 * j, :] = adj[q]
         return carry
 
-    lax.fori_loop(0, OCT * 2, finish, 0)
+    lax.fori_loop(0, OCT, finish, 0)
     snap_ref[...] = packed[...].astype(BF16)
     pay_ref[...] = paysum[...].astype(BF16)
     for j in range(2):
@@ -343,26 +367,29 @@
         total = total + dot(one_hot, cgrad[:, i, :].astype(BF16), ((1,), (1,)))
     packed[0, :, :] = jnp.zeros((ROWS, COLS), F32)
     packed[0, 0:CLASSES, 0:OUTS] = total
-    sums_ref[...] = packed[0, 0:8, :] + turn(packed[0, 8:16, :], 32)
+    parts = [packed[0, 4 * q : 4 * q + 4, :] for q in range(4)]
+    sums_ref[...] = (parts[0] + turn(parts[1], 32)) + (turn(parts[2], 64) + turn(parts[3], 96))
 
 
 def last_kernel(parts_ref, scale_ref, f_ref, h1_ref, h2_ref, w1_ref, w2_ref, w3_ref,
-                embed_ref, time_ref, one_ref, two_ref, three_ref, *, factor):
+                embed_ref, time_ref, one_ref, two_ref, three_ref, classed, *, factor):
     total = parts_ref[0]
     for i in range(1, parts_ref.shape[0]):
         total = total + parts_ref[i]
     total = total * factor
-    sums = jnp.concatenate([total[:, 0:OUTS], turn(total, -32)[:, 0:OUTS]], axis=0)
+    for q in range(4):
+        classed[4 * q : 4 * q + 4, :] = turn(total, -32 * q)
+    sums = classed[:, 0:OUTS]
     f, h1, h2 = f_ref[...], h1_ref[...], h2_ref[...]
-    two_grad = dot(sums, w3_ref[...].astype(F32), ((1,), (1,)), HIGHEST) * (1.0 - h2 * h2)
+    two_grad = dot(sums, w3_ref[...].astype(F32), ((1,), (0,)), HIGHEST) * (1.0 - h2 * h2)
     one_grad = dot(two_grad, w2_ref[...].astype(F32), ((1,), (1,)), HIGHEST) * (1.0 - h1 * h1)
     feature_grad = dot(one_grad, w1_ref[...].astype(F32), ((1,), (1,)), HIGHEST)
-    three_ref[...] = dot(h2, sums, ((0,), (0,)), HIGHEST)
+    three_ref[...] = dot(sums, h2, ((0,), (0,)), HIGHEST)
     two_ref[...] = dot(h1, two_grad, ((0,), (0,)), HIGHEST)
     one_ref[...] = dot(f, one_grad, ((0,), (0,)), HIGHEST)
     embed_ref[...] = feature_grad
     scale = scale_ref[...].astype(F32) * (1.0 / 64.0)
-    time_ref[...] = scale * jnp.sum(feature_grad, axis=0, keepdims=True)
+    time_ref[...] = scale[0] * jnp.sum(feature_grad, axis=0)
 
 
 def shift(x, axis, step):
@@ -378,14 +405,17 @@
 
 def body(classes, check_index, snapshot, payoff, sensitivity, embed, time_vec, w_one, w_two, w_three):
     sd = jax.ShapeDtypeStruct
-    marked = (classes + 1).astype(BF16)
-
-    def edge_rows(v, r, s, c):
-        c = jnp.pad(c[:, None, :], ((0, GOALS - RH), (0, 1), (0, 0)))
-        return jnp.concatenate([v, r, s, c], axis=1)
-
-    to_down = edge_rows(snapshot[:, -VH:], payoff[:, -RH:], sensitivity[:, -FH:], marked[-RH:])
-    to_up = edge_rows(snapshot[:, :VH], payoff[:, :RH], sensitivity[:, :FH], marked[:RH])
+    tile = sd((GOALS, ROWS, COLS), BF16)
+    to_down, to_up = vmem_call(
+        edge_kernel,
+        (tile, tile),
+        [pltpu.VMEM((ROWS, COLS), F32)] * 2
+        + [pltpu.VMEM((GOALS, ROWS, COLS), BF16)] * 3
+        + [pltpu.VMEM((ROWS, COLS), jnp.int32), pltpu.SemaphoreType.DMA((4,))],
+        source=pl.ANY,
+    )(
+        snapshot, payoff, sensitivity, classes
+    )
     up = shift(to_down, "row", 1)
     down = shift(to_up, "row", -1)
 
@@ -393,18 +423,17 @@
     layer = sd((CLASSES, 64), F32)
     table, feature, one, two = vmem_call(
         table_kernel, (sd((72, COLS), F32), layer, layer, layer), [pltpu.VMEM((32, COLS), F32)]
-    )(scale, embed, time_vec.reshape(1, -1), w_one, w_two, w_three)
+    )(scale, embed, time_vec.reshape(1, -1), w_one, w_two, w_three.T)
 
     ext = pltpu.VMEM((GOALS, EXT, COLS), F32)
     plane = pltpu.VMEM((EXT, COLS), F32)
-    edge = sd((OCT + 1, 32, COLS), F32)
+    edge = sd((OCT + 1, 32, COLS), BF16)
     to_right, to_left = vmem_call(strip_kernel, (edge, edge), [ext, ext, ext, plane])(
         snapshot, payoff, sensitivity, classes, up, down
     )
-    left = shift(to_right.astype(BF16), "col", 1)
-    right = shift(to_left.astype(BF16), "col", -1)
-
-    tile = sd((GOALS, ROWS, COLS), BF16)
+    left = shift(to_right, "col", 1)
+    right = shift(to_left, "col", -1)
+
     strip = pltpu.VMEM((OCT, EXT, COLS), F32)
 
     def many(*shape):
@@ -413,7 +442,7 @@
     n = ACTIONS * POINTS
     snap, pay, sums = vmem_call(
         main_kernel,
-        (tile, tile, sd((8, COLS), F32)),
+        (tile, tile, sd((4, COLS), F32)),
         [
             many(ITERS, GOALS, EXT), ext, ext, plane,
             many(ITERS, OCT, EXT), strip, strip, plane,
@@ -433,9 +462,10 @@
         last_kernel(*refs, factor=factor)
 
     grads = vmem_call(
-        last, (layer, sd((1, 64), F32), sd((64, 64), F32), sd((64, 64), F32), sd((64, OUTS), F32))
-    )(parts, scale, feature, one, two, w_one, w_two, w_three)
-    return (snap, pay, grads[0], grads[1].reshape(64), grads[2], grads[3], grads[4])
+        last, (layer, sd((64,), F32), sd((64, 64), F32), sd((64, 64), F32), sd((OUTS, 64), F32)),
+        [pltpu.VMEM((CLASSES, COLS), F32)],
+    )(parts, scale, feature, one, two, w_one, w_two, w_three.T)
+    return (snap, pay, grads[0], grads[1], grads[2], grads[3], grads[4].T)
 
 
 def solution(mesh):

time: 97.3 us -> 81.3 us (0.84)
  Pallas kernels: 26.7 us -> 13.3 us
  blocking collectives: 46 us -> 43.7 us
    pallas_call x4 -> x5, Pallas kernels: 26.7 us -> 13.3 us  [vmem_call(): pl.pallas_call(kernel, out_shape=out_shape, in_specs=[given] * len(args),...]
    all_to_all x2, blocking collectives: 46 us -> 43.7 us  [spread(): lax.all_to_all(jnp.broadcast_to(x[None], (size,) + x.shape), axis, 0, 0,...]
    unnamed x20 -> x22, local copies, waits for them, and re-layouts: 2.31 us -> 4.03 us
  transfers between devices with their start and end apart: 4 -> 4, of which waited for: 2 -> 3; matrix products, arithmetic and copies ran while one was open for 0% -> 0% of each run, Pallas kernels for 0% -> 1%
where the time goes in v2:
time: 81.3 us; the launch traced here: 80.8 us
  blocking collectives  43.7 us (54%)
  starting transfers between devices  13.8 us (17%)
  Pallas kernels  13.3 us (16%)
  waiting for transfers between devices  4.57 us (6%)
  local copies, waits for them, and re-layouts  4.05 us (5%)
  between operations  1.42 us (2%)
    all_to_all x2, blocking collectives, spread(): lax.all_to_all(jnp.broadcast_to(x[None], (size,) + x.shape), axis, 0, 0,...  43.7 us
    ppermute x4, starting transfers between devices, shift(): return lax.ppermute(x, axis, pairs)  13.8 us
    pallas_call x5, Pallas kernels, vmem_call(): pl.pallas_call(kernel, out_shape=out_shape, in_specs=[given] * len(args),...  13.3 us
    ppermute x4, waiting for transfers between devices, shift(): return lax.ppermute(x, axis, pairs)  4.57 us
    unnamed x22, local copies, waits for them, and re-layouts  4.03 us
  transfers between devices with their start and end apart: 4, of which 3 were waited for; matrix products, arithmetic and copies ran while one was open for 0% of the time, Pallas kernels for 1%

profile of v2, /device:TPU:1, one launch (start us, length us, event | category | flops | bytes accessed | tf_op | source)
XLA Modules:
  0.0 80.8 jit_solution(11342445318146462454)
XLA Ops:
  0.6 0.0 copy-start
  0.6 0.9 %copy-done = bf16[24,16,128]{2,1,0:T(8,128)(2,1)S(1)} copy-done((bf16[24,16,128]{2,1,0:T(8,128)(2,1)S(1)}, bf16[24,16,128]{2,1,0:T(8,128)(2,1)}, u32[]{:S(2)}) %copy-start) | copy-done | bytes 98328
  1.5 0.9 %copy-done.2 = bf16[24,16,128]{2,1,0:T(8,128)(2,1)S(1)} copy-done((bf16[24,16,128]{2,1,0:T(8,128)(2,1)S(1)}, bf16[24,16,128]{2,1,0:T(8,128)(2,1)}, u32[]{:S(2)}) %copy-start.2) | copy-done | bytes 98328
  2.4 0.9 %copy-done.4 = bf16[24,16,128]{2,1,0:T(8,128)(2,1)S(1)} copy-done((bf16[24,16,128]{2,1,0:T(8,128)(2,1)S(1)}, bf16[24,16,128]{2,1,0:T(8,128)(2,1)}, u32[]{:S(2)}) %copy-start.4) | copy-done | bytes 98328
  3.3 0.7 copy-done.5
  4.0 0.5 shard_map.153
  4.6 4.0 %collective-permute-start = (bf16[24,16,128]{2,1,0:T(8,128)(2,1)S(1)}, bf16[24,16,128]{2,1,0:T(8,128)(2,1)S(1)}, u32[]{:S(2)}, u32[]{:S(2)}) collective-permute-start(bf16[24,16,128]{2,1,0:T(8,128)(2,1)S(1)} %get-tuple-element.23), channel_id=1, source_target_pairs={{0,32},{32,64},{64,96},{96,128},{128,160},{160,192},{192,224},{224... | collective-permute-start | bytes 294920 | tf_op jit(solution)/shard_map/ppermute | solution.py:398
  8.6 1.3 %collective-permute-start.1 = (bf16[24,16,128]{2,1,0:T(8,128)(2,1)S(1)}, bf16[24,16,128]{2,1,0:T(8,128)(2,1)S(1)}, u32[]{:S(2)}, u32[]{:S(2)}) collective-permute-start(bf16[24,16,128]{2,1,0:T(8,128)(2,1)S(1)} %get-tuple-element.24), channel_id=1, source_target_pairs={{32,0},{64,32},{96,64},{128,96},{160,128},{192,160},{224,192},{256... | collective-permute-start | bytes 294920 | tf_op jit(solution)/shard_map/ppermute | solution.py:398
  9.9 0.3 collective-permute-done.up_ref
  10.2 3.7 %collective-permute-done.1.down_ref = bf16[24,16,128]{2,1,0:T(8,128)(2,1)S(1)} collective-permute-done((bf16[24,16,128]{2,1,0:T(8,128)(2,1)S(1)}, bf16[24,16,128]{2,1,0:T(8,128)(2,1)S(1)}, u32[]{:S(2)}, u32[]{:S(2)}) %collective-permute-start.1) | collective-permute-done | bytes 98336 | tf_op jit(solution)/shard_map/ppermute | solution.py:398
  14.0 0.7 shard_map.154
  14.7 0.0 copy-start.8
  14.7 5.5 %collective-permute-start.2 = (bf16[4,32,128]{2,1,0:T(8,128)(2,1)S(1)}, bf16[4,32,128]{2,1,0:T(8,128)(2,1)S(1)}, u32[]{:S(2)}, u32[]{:S(2)}) collective-permute-start(bf16[4,32,128]{2,1,0:T(8,128)(2,1)S(1)} %get-tuple-element.25), channel_id=1, source_target_pairs={{0,1},{1,2},{2,3},{3,4},{4,5},{5,6},{6,7},{7,8},{8,9},{9,10},{10,1... | collective-permute-start | bytes 98312 | tf_op jit(solution)/shard_map/ppermute | solution.py:398
  20.3 3.0 %collective-permute-start.3 = (bf16[4,32,128]{2,1,0:T(8,128)(2,1)S(1)}, bf16[4,32,128]{2,1,0:T(8,128)(2,1)S(1)}, u32[]{:S(2)}, u32[]{:S(2)}) collective-permute-start(bf16[4,32,128]{2,1,0:T(8,128)(2,1)S(1)} %get-tuple-element.26), channel_id=1, source_target_pairs={{1,0},{2,1},{3,2},{4,3},{5,4},{6,5},{7,6},{8,7},{9,8},{10,9},{11,1... | collective-permute-start | bytes 98312 | tf_op jit(solution)/shard_map/ppermute | solution.py:398
  23.9 0.0 copy-start.9
  23.9 0.0 copy-start.10
  23.9 0.6 copy-done.9
  24.6 0.4 shard_map.155
  25.0 0.0 collective-permute-done.2.lb_ref
  25.0 0.5 collective-permute-done.3.rb_ref
  25.5 10.3 %shard_map.156 = (bf16[24,16,128]{2,1,0:T(8,128)(2,1)}, bf16[24,16,128]{2,1,0:T(8,128)(2,1)}, f32[4,128]{1,0:T(4,128)S(1)}) custom-call(bf16[24,16,128]{2,1,0:T(8,128)(2,1)S(1)} %copy-done.1, bf16[24,16,128]{2,1,0:T(8,128)(2,1)S(1)} %copy-done.3, bf16[24,16,128]{2,1,0:T(8,128)(2,1)S(1)} %copy-done.4, s32[16,128]{1,0:T(8,128)S(1)} %copy-done.5, ...), custom_call_target="tpu_custom_call" | custom-call | tf_op jit(solution)/shard_map/pallas_call | solution.py:33
  35.8 14.2 %all_to_all.10 = f32[16,4,128]{2,1,0:T(4,128)S(1)} all-to-all(f32[16,4,128]{2,1,0:T(4,128)S(1)} %broadcast_in_dim.10), channel_id=1, replica_groups=mesh['row'=16,'col'=32] {'row'}, dimensions={0} | all-to-all | bytes 65536 | tf_op jit(solution)/shard_map/all_to_all | solution.py:403
  50.0 29.5 %all_to_all.11.refs_0_ = f32[32,4,128]{2,1,0:T(4,128)S(1)} all-to-all(f32[32,4,128]{2,1,0:T(4,128)S(1)} %broadcast_in_dim.22), channel_id=1, replica_groups=mesh['row'=16,'col'=32] {'col'}, dimensions={0} | all-to-all | bytes 131072 | tf_op jit(solution)/shard_map/all_to_all | solution.py:403
  79.5 1.3 %shard_map.157 = (f32[16,64]{1,0:T(8,128)}, f32[64]{0:T(128)}, f32[64,64]{1,0:T(8,128)}, f32[64,64]{1,0:T(8,128)}, f32[24,64]{1,0:T(8,128)}) custom-call(f32[32,4,128]{2,1,0:T(4,128)S(1)} %all_to_all.11.refs_0_, s32[1,64]{1,0:T(1,128)S(1)} %broadcast_in_dim.9.scale_ref.refs_1_, f32[16,64]{1,0:T(8,128)S(1)} %get-tuple-element.31.refs_2_, ...), custom_call_target="tpu_custom_call" | custom-call | tf_op jit(solution)/shard_map/pallas_call | solution.py:33
  (17 shorter events, 0.1 us)
Async XLA Ops:
  0.6 0.9 %copy-start = (bf16[24,16,128]{2,1,0:T(8,128)(2,1)S(1)}, bf16[24,16,128]{2,1,0:T(8,128)(2,1)}, u32[]{:S(2)}) copy-start(bf16[24,16,128]{2,1,0:T(8,128)(2,1)} %v_ref.3) | copy-start | bytes 294916
  1.5 0.9 %copy-start.2 = (bf16[24,16,128]{2,1,0:T(8,128)(2,1)S(1)}, bf16[24,16,128]{2,1,0:T(8,128)(2,1)}, u32[]{:S(2)}) copy-start(bf16[24,16,128]{2,1,0:T(8,128)(2,1)} %r_ref.3) | copy-start | bytes 294916
  2.4 0.9 %copy-start.4 = (bf16[24,16,128]{2,1,0:T(8,128)(2,1)S(1)}, bf16[24,16,128]{2,1,0:T(8,128)(2,1)}, u32[]{:S(2)}) copy-start(bf16[24,16,128]{2,1,0:T(8,128)(2,1)} %s_ref.3) | copy-start | bytes 294916
  3.3 0.7 copy-start.5
  4.6 5.7 %collective-permute-start = (bf16[24,16,128]{2,1,0:T(8,128)(2,1)S(1)}, bf16[24,16,128]{2,1,0:T(8,128)(2,1)S(1)}, u32[]{:S(2)}, u32[]{:S(2)}) collective-permute-start(bf16[24,16,128]{2,1,0:T(8,128)(2,1)S(1)} %get-tuple-element.23), channel_id=1, source_target_pairs={{0,32},{32,64},{64,96},{96,128},{128,160},{160,192},{192,224},{224... | collective-permute-start | bytes 294920 | tf_op jit(solution)/shard_map/ppermute | solution.py:398
  8.6 5.4 %collective-permute-start.1 = (bf16[24,16,128]{2,1,0:T(8,128)(2,1)S(1)}, bf16[24,16,128]{2,1,0:T(8,128)(2,1)S(1)}, u32[]{:S(2)}, u32[]{:S(2)}) collective-permute-start(bf16[24,16,128]{2,1,0:T(8,128)(2,1)S(1)} %get-tuple-element.24), channel_id=1, source_target_pairs={{32,0},{64,32},{96,64},{128,96},{160,128},{192,160},{224,192},{256... | collective-permute-start | bytes 294920 | tf_op jit(solution)/shard_map/ppermute | solution.py:398
  14.0 9.9 %copy-start.6 = (bf16[64,64]{1,0:T(8,128)(2,1)S(1)}, bf16[64,64]{1,0:T(8,128)(2,1)}, u32[]{:S(2)}) copy-start(bf16[64,64]{1,0:T(8,128)(2,1)} %refs_5_.1) | copy-start | bytes 24580
  14.0 9.9 %copy-start.7 = (bf16[64,64]{1,0:T(8,128)(2,1)S(1)}, bf16[64,64]{1,0:T(8,128)(2,1)}, u32[]{:S(2)}) copy-start(bf16[64,64]{1,0:T(8,128)(2,1)} %refs_6_.1) | copy-start | bytes 24580
  14.0 11.5 %copy-start.1 = (bf16[24,16,128]{2,1,0:T(8,128)(2,1)S(1)}, bf16[24,16,128]{2,1,0:T(8,128)(2,1)}, u32[]{:S(2)}) copy-start(bf16[24,16,128]{2,1,0:T(8,128)(2,1)} %v_ref.3) | copy-start | bytes 294916
  14.0 11.5 %copy-start.3 = (bf16[24,16,128]{2,1,0:T(8,128)(2,1)S(1)}, bf16[24,16,128]{2,1,0:T(8,128)(2,1)}, u32[]{:S(2)}) copy-start(bf16[24,16,128]{2,1,0:T(8,128)(2,1)} %r_ref.3) | copy-start | bytes 294916
  14.7 9.2 %copy-start.8 = (bf16[64,24]{0,1:T(8,128)(2,1)S(1)}, bf16[64,24]{0,1:T(8,128)(2,1)}, u32[]{:S(2)}) copy-start(bf16[64,24]{0,1:T(8,128)(2,1)} %param.19) | copy-start | bytes 9220
  14.7 10.3 %collective-permute-start.2 = (bf16[4,32,128]{2,1,0:T(8,128)(2,1)S(1)}, bf16[4,32,128]{2,1,0:T(8,128)(2,1)S(1)}, u32[]{:S(2)}, u32[]{:S(2)}) collective-permute-start(bf16[4,32,128]{2,1,0:T(8,128)(2,1)S(1)} %get-tuple-element.25), channel_id=1, source_target_pairs={{0,1},{1,2},{2,3},{3,4},{4,5},{5,6},{6,7},{7,8},{8,9},{9,10},{10,1... | collective-permute-start | bytes 98312 | tf_op jit(solution)/shard_map/ppermute | solution.py:398
  20.3 5.2 %collective-permute-start.3 = (bf16[4,32,128]{2,1,0:T(8,128)(2,1)S(1)}, bf16[4,32,128]{2,1,0:T(8,128)(2,1)S(1)}, u32[]{:S(2)}, u32[]{:S(2)}) collective-permute-start(bf16[4,32,128]{2,1,0:T(8,128)(2,1)S(1)} %get-tuple-element.26), channel_id=1, source_target_pairs={{1,0},{2,1},{3,2},{4,3},{5,4},{6,5},{7,6},{8,7},{9,8},{10,9},{11,1... | collective-permute-start | bytes 98312 | tf_op jit(solution)/shard_map/ppermute | solution.py:398
  23.9 0.7 copy-start.9
  23.9 0.7 copy-start.10

commit v3 on v2

--- a/solution.py
+++ b/solution.py
@@ -27,7 +27,7 @@
 BF16 = jnp.bfloat16
 
 
-def vmem_call(kernel, out_shape, scratch=(), limit=48 * 1024 * 1024, source=pltpu.VMEM):
+def vmem_call(kernel, out_shape, scratch=(), limit=40 * 1024 * 1024, source=pltpu.VMEM):
     whole = pl.BlockSpec(memory_space=pltpu.VMEM)
     given = pl.BlockSpec(memory_space=source)
     return lambda *args: pl.pallas_call(
@@ -40,6 +40,14 @@
     )(*args)
 
 
+def fetch(pairs, sems):
+    copies = [pltpu.make_async_copy(a, b, sems.at[i]) for i, (a, b) in enumerate(pairs)]
+    for copy in copies:
+        copy.start()
+    for copy in copies:
+        copy.wait()
+
+
 def lane_iota(shape):
     return lax.broadcasted_iota(jnp.int32, shape, len(shape) - 1)
 
@@ -53,7 +61,10 @@
     return lax.dot_general(a, b, (dims, ((), ())), precision=precision, preferred_element_type=F32)
 
 
-def table_kernel(scale_ref, embed_ref, time_ref, w1_ref, w2_ref, w3_ref, tab_ref, f_ref, h1_ref, h2_ref, raw):
+def table_kernel(scale_hbm, embed_hbm, time_hbm, w1_hbm, w2_hbm, w3_hbm, tab_ref, f_ref, h1_ref, h2_ref,
+                 scale_ref, w1_ref, w2_ref, w3_ref, raw, embed_ref, time_ref, sems):
+    fetch(((scale_hbm, scale_ref), (embed_hbm, embed_ref), (time_hbm, time_ref),
+           (w1_hbm, w1_ref), (w2_hbm, w2_ref), (w3_hbm, w3_ref)), sems)
     scale = scale_ref[...].astype(F32) * (1.0 / 64.0)
     feature = (embed_ref[...].astype(F32) + scale * time_ref[...].astype(F32)).astype(BF16)
     one = jnp.tanh(dot(feature, w1_ref[...], ((1,), (0,)))).astype(BF16)
@@ -88,18 +99,12 @@
     return 64 + a
 
 
-def edge_kernel(v_hbm, r_hbm, s_hbm, c_hbm, to_down, to_up, low, high, v_ref, r_ref, s_ref, c_ref, sems):
-    pairs = ((v_hbm, v_ref), (r_hbm, r_ref), (s_hbm, s_ref), (c_hbm, c_ref))
-    copies = [pltpu.make_async_copy(a, b, sems.at[i]) for i, (a, b) in enumerate(pairs)]
-    for copy in copies:
-        copy.start()
-    for copy in copies:
-        copy.wait()
+def edge_kernel(all_ref, to_down, to_up, low, high):
     low[...] = jnp.zeros_like(low)
     high[...] = jnp.zeros_like(high)
-    marked = c_ref[...].astype(F32) + 1.0
+    marked = all_ref[3 * GOALS].astype(F32)
     for g in range(GOALS):
-        v, r, s = v_ref[g].astype(F32), r_ref[g].astype(F32), s_ref[g].astype(F32)
+        v, r, s = [all_ref[i * GOALS + g].astype(F32) for i in range(3)]
         low[0:6, :], low[6:11, :], low[11:14, :] = v[ROWS - VH :], r[ROWS - RH :], s[ROWS - FH :]
         high[0:6, :], high[6:11, :], high[11:14, :] = v[0:VH], r[0:RH], s[0:FH]
         if g < RH:
@@ -114,25 +119,25 @@
     dst[g, TOP + ROWS : TOP + ROWS + n, :] = down
 
 
-def extend_rows(v_ref, r_ref, s_ref, c_ref, up_ref, down_ref, val, rew, sen, cls):
+def extend_rows(all_ref, up_ref, down_ref, val, rew, sen, cls):
     def one(g, carry):
         up = up_ref[g].astype(F32)
         down = down_ref[g].astype(F32)
-        fill_rows(val, g, up[0:6], v_ref[g].astype(F32), down[0:6], VH)
-        fill_rows(rew, g, up[6:11], r_ref[g].astype(F32), down[6:11], RH)
-        fill_rows(sen, g, up[11:14], s_ref[g].astype(F32), down[11:14], FH)
+        fill_rows(val, g, up[0:6], all_ref[g].astype(F32), down[0:6], VH)
+        fill_rows(rew, g, up[6:11], all_ref[GOALS + g].astype(F32), down[6:11], RH)
+        fill_rows(sen, g, up[11:14], all_ref[2 * GOALS + g].astype(F32), down[11:14], FH)
         return carry
 
     lax.fori_loop(0, GOALS, one, 0, unroll=4)
     cls[...] = jnp.zeros_like(cls)
-    cls[TOP : TOP + ROWS, :] = c_ref[...].astype(F32) + 1.0
+    cls[TOP : TOP + ROWS, :] = all_ref[3 * GOALS].astype(F32)
     for i in range(RH):
         cls[TOP - RH + i : TOP - RH + i + 1, :] = up_ref[i, 14:15, :].astype(F32)
         cls[TOP + ROWS + i : TOP + ROWS + i + 1, :] = down_ref[i, 14:15, :].astype(F32)
 
 
-def strip_kernel(v_ref, r_ref, s_ref, c_ref, up_ref, down_ref, to_right, to_left, val, rew, sen, cls):
-    extend_rows(v_ref, r_ref, s_ref, c_ref, up_ref, down_ref, val, rew, sen, cls)
+def strip_kernel(all_ref, up_ref, down_ref, tab_ref, to_right, to_left, val, rew, sen, cls):
+    extend_rows(all_ref, up_ref, down_ref, val, rew, sen, cls)
     group_lane = lane_iota((8, COLS)) % GROUP
     group_at = lane_iota((8, COLS)) // GROUP
 
@@ -166,12 +171,35 @@
         to_left[OCT, 8 * j : 8 * j + 8, :] = left.astype(to_left.dtype)
 
 
-def main_kernel(v_ref, r_ref, s_ref, c_ref, up_ref, down_ref, lb_ref, rb_ref, tab_ref,
+def look_up(base, cls, tab_ref, chance, bonus, mask, slope=None):
+    at = slice(base, base + 8)
+    number = cls[at, :].astype(jnp.int32)
+    inside = number > 0
+    which = jnp.maximum(number - 1, 0)
+    mask[at, :] = inside.astype(F32)
+
+    def look(row):
+        table = jnp.broadcast_to(tab_ref[row : row + 1, :], (8, COLS))
+        return jnp.where(inside, jnp.take_along_axis(table, which, axis=1), 0.0)
+
+    for a in range(ACTIONS):
+        for k in range(POINTS):
+            chance[a * POINTS + k, at, :] = look(chance_row(a, k))
+            if slope is not None:
+                slope[a * POINTS + k, base - TOP : base - TOP + 8, :] = look(slope_row(a, k))
+        bonus[a, at, :] = look(bonus_row(a))
+
+
+def map_kernel(cls, tab_ref, chance, bonus, mask, slope):
+    for j in range(4):
+        look_up(8 + 8 * j, cls, tab_ref, chance, bonus, mask, slope if j in (1, 2) else None)
+
+
+def main_kernel(val0, rew, sen, cls, chance, bonus, mask, slope, lb_ref, rb_ref, tab_ref,
                 snap_ref, pay_ref, sums_ref,
-                val, rew, sen, cls, sval, srew, ssen, scls,
-                chance, schance, bonus, sbonus, mask, smask, slope,
-                soft, ssoft, lshift, rshift, push, spush, cgrad, paysum, packed):
-    extend_rows(v_ref, r_ref, s_ref, c_ref, up_ref, down_ref, val.at[0], rew, sen, cls)
+                later, sval, srew, ssen, scls, schance, sbonus, smask,
+                soft, ssoft, lshift, rshift, push, spush, adjoint, cgrad, paysum, packed):
+    val = [val0, later.at[0], later.at[1]]
     lane = lane_iota((8, COLS))
     glane = lane % GROUP
     inner = glane < 6
@@ -190,26 +218,10 @@
                 srew[o, at, :] = jnp.where(inner, turn(left, -5), right)
                 ssen[o, at, :] = jnp.where(inner, turn(left, -8), turn(right, -5))
     for j in range(4):
-        at = slice(8 + 8 * j, 16 + 8 * j)
-        for source, ch, bo, ma in ((cls, chance, bonus, mask), (scls, schance, sbonus, smask)):
-            number = source[at, :].astype(jnp.int32)
-            inside = number > 0
-            which = jnp.maximum(number - 1, 0)
-            ma[at, :] = inside.astype(F32)
-
-            def look(row):
-                table = jnp.broadcast_to(tab_ref[row : row + 1, :], (8, COLS))
-                return jnp.where(inside, jnp.take_along_axis(table, which, axis=1), 0.0)
-
-            for a in range(ACTIONS):
-                for k in range(POINTS):
-                    ch[a * POINTS + k, at, :] = look(chance_row(a, k))
-                    if source is cls and j in (1, 2):
-                        slope[a * POINTS + k, 8 * j - 8 : 8 * j, :] = look(slope_row(a, k))
-                bo[a, at, :] = look(bonus_row(a))
-
-    def where_tile(j):
-        base = 8 + 8 * j
+        look_up(8 + 8 * j, scls, tab_ref, schance, sbonus, smask)
+
+    def where_tile(start):
+        base = TOP + start
         return slice(base, base + 8), slice(base - 1, base + 7), slice(base + 1, base + 9)
 
     def soft_step(near, reward, ch, bo, keep_value):
@@ -229,27 +241,27 @@
     for t in range(ITERS):
         keep = t < ITERS - 1
 
-        def forward(o, j, t=t, keep=keep):
-            rows, above, below = where_tile(j)
+        def forward(o, start, t=t, keep=keep):
+            rows, above, below = where_tile(start)
             ch = [chance[n, rows, :] for n in range(ACTIONS * POINTS)]
             bo = [bonus[a, rows, :] for a in range(ACTIONS)]
             sv = sval[t, o, rows, :]
             edge = jnp.zeros((8, COLS), F32)
             for q in range(8):
                 p, g = GROUP * q, o * 8 + q
-                x = val[t, g, rows, :]
+                x = val[t][g, rows, :]
                 fill = turn(sv, -(p + 6))
                 toleft = turn(jnp.where(last, fill, x), 1)
                 toright = turn(jnp.where(first, fill, x), -1)
                 edge = jnp.where((lane == p + 5) | (lane == p + 6), turn(x, p + 6), edge)
                 lshift[t, g, rows, :] = toleft
                 rshift[t, g, rows, :] = toright
-                near = [x, val[t, g, above, :], val[t, g, below, :], toleft, toright]
+                near = [x, val[t][g, above, :], val[t][g, below, :], toleft, toright]
                 probs, value = soft_step(near, rew[g, rows, :], ch, bo, keep)
                 for a in range(ACTIONS):
                     soft[t, a, g, rows, :] = probs[a]
                 if keep:
-                    val[t + 1, g, rows, :] = value * mask[rows, :]
+                    val[t + 1][g, rows, :] = value * mask[rows, :]
             near = [sv, sval[t, o, above, :], sval[t, o, below, :],
                     turn(jnp.where(strip_first, edge, sv), 1), turn(jnp.where(strip_last, edge, sv), -1)]
             ch = [schance[n, rows, :] for n in range(ACTIONS * POINTS)]
@@ -260,9 +272,11 @@
             if keep:
                 sval[t + 1, o, rows, :] = value * smask[rows, :]
 
-        def forward_all(o, carry, forward=forward):
-            for j in range(4):
-                forward(o, j)
+        starts = (-6, 2, 10, 18) if t == 0 else (-4, 4, 12)
+
+        def forward_all(o, carry, forward=forward, starts=starts):
+            for start in starts:
+                forward(o, start)
             return carry
 
         lax.fori_loop(0, OCT, forward_all, 0)
@@ -291,13 +305,15 @@
     for t in reversed(range(ITERS)):
         new, old = t % 2, (t + 1) % 2
 
-        def backward(o, j, own, t=t, new=new, old=old):
-            rows, above, below = where_tile(j)
+        def spread_out(o, start, t=t, new=new, old=old):
+            rows, above, below = where_tile(start)
             if t == ITERS - 1:
                 adj = [sen[o * 8 + q, rows, :] for q in range(8)]
                 strip = ssen[o, rows, :]
             else:
                 adj, strip = gather(o, rows, above, below, old)
+                for q in range(8):
+                    adjoint[o * 8 + q, rows, :] = adj[q]
             for q in range(8):
                 g = o * 8 + q
                 grads = [adj[q] * soft[t, a, g, rows, :] for a in range(ACTIONS)]
@@ -306,25 +322,6 @@
                     for a in range(1, ACTIONS):
                         total = total + grads[a] * chance[a * POINTS + k, rows, :]
                     push[new, k, g, rows, :] = total
-            if own:
-                at = slice(8 * j - 8, 8 * j)
-                for q in range(8):
-                    g = o * 8 + q
-                    grads = [adj[q] * soft[t, a, g, rows, :] for a in range(ACTIONS)]
-                    paysum[g, at, :] += (grads[0] + grads[1]) + (grads[2] + grads[3])
-                for a in range(ACTIONS):
-                    sums = [cgrad[a * POINTS + k, at, :] for k in range(POINTS)]
-                    total = cgrad[ACTIONS * POINTS + a, at, :]
-                    for q in range(8):
-                        g = o * 8 + q
-                        grad = adj[q] * soft[t, a, g, rows, :]
-                        total = total + grad
-                        near = [val[t, g, rows, :], val[t, g, above, :], val[t, g, below, :],
-                                lshift[t, g, rows, :], rshift[t, g, rows, :]]
-                        sums = [x + grad * y for x, y in zip(sums, near)]
-                    for k in range(POINTS):
-                        cgrad[a * POINTS + k, at, :] = sums[k]
-                    cgrad[ACTIONS * POINTS + a, at, :] = total
             grads = [strip * ssoft[t, a, o, rows, :] for a in range(ACTIONS)]
             for k in range(POINTS):
                 total = grads[0] * schance[k, rows, :]
@@ -332,19 +329,44 @@
                     total = total + grads[a] * schance[a * POINTS + k, rows, :]
                 spush[new, k, o, rows, :] = total
 
-        def backward_all(o, carry, backward=backward):
-            for j in range(4):
-                backward(o, j, j in (1, 2))
+        def collect(o, start, t=t):
+            rows, above, below = where_tile(start)
+            source = sen if t == ITERS - 1 else adjoint
+            adj = [source[o * 8 + q, rows, :] for q in range(8)]
+            at = slice(start, start + 8)
+            for q in range(8):
+                g = o * 8 + q
+                grads = [adj[q] * soft[t, a, g, rows, :] for a in range(ACTIONS)]
+                paysum[g, at, :] += (grads[0] + grads[1]) + (grads[2] + grads[3])
+            for a in range(ACTIONS):
+                sums = [cgrad[a * POINTS + k, at, :] for k in range(POINTS)]
+                total = cgrad[ACTIONS * POINTS + a, at, :]
+                for q in range(8):
+                    g = o * 8 + q
+                    grad = adj[q] * soft[t, a, g, rows, :]
+                    total = total + grad
+                    near = [val[t][g, rows, :], val[t][g, above, :], val[t][g, below, :],
+                            lshift[t, g, rows, :], rshift[t, g, rows, :]]
+                    sums = [x + grad * y for x, y in zip(sums, near)]
+                for k in range(POINTS):
+                    cgrad[a * POINTS + k, at, :] = sums[k]
+                cgrad[ACTIONS * POINTS + a, at, :] = total
+
+        def backward_all(o, carry, spread_out=spread_out, collect=collect):
+            for start in (-4, 4, 12):
+                spread_out(o, start)
+            for start in (0, 8):
+                collect(o, start)
             return carry
 
         lax.fori_loop(0, OCT, backward_all, 0)
 
     def finish(o, carry):
-        for j in (1, 2):
-            rows, above, below = where_tile(j)
+        for start in (0, 8):
+            rows, above, below = where_tile(start)
             adj = gather(o, rows, above, below, 0)[0]
             for q in range(8):
-                packed[o * 8 + q, 8 * j - 8 : 8 * j, :] = adj[q]
+                packed[o * 8 + q, start : start + 8, :] = adj[q]
         return carry
 
     lax.fori_loop(0, OCT, finish, 0)
@@ -362,8 +384,9 @@
                 cgrad[a * POINTS + k, at, :] = (DECAY * grads[k] - weighted) * slope[a * POINTS + k, at, :]
     number = lax.broadcasted_iota(jnp.int32, (CLASSES, COLS), 0)
     total = jnp.zeros((CLASSES, OUTS), F32)
+    which = cls[TOP : TOP + ROWS, :].astype(jnp.int32) - 1
     for i in range(ROWS):
-        one_hot = (number == c_ref[i : i + 1, :]).astype(BF16)
+        one_hot = (number == which[i : i + 1]).astype(BF16)
         total = total + dot(one_hot, cgrad[:, i, :].astype(BF16), ((1,), (1,)))
     packed[0, :, :] = jnp.zeros((ROWS, COLS), F32)
     packed[0, 0:CLASSES, 0:OUTS] = total
@@ -406,31 +429,29 @@
 def body(classes, check_index, snapshot, payoff, sensitivity, embed, time_vec, w_one, w_two, w_three):
     sd = jax.ShapeDtypeStruct
     tile = sd((GOALS, ROWS, COLS), BF16)
-    to_down, to_up = vmem_call(
-        edge_kernel,
-        (tile, tile),
-        [pltpu.VMEM((ROWS, COLS), F32)] * 2
-        + [pltpu.VMEM((GOALS, ROWS, COLS), BF16)] * 3
-        + [pltpu.VMEM((ROWS, COLS), jnp.int32), pltpu.SemaphoreType.DMA((4,))],
-        source=pl.ANY,
-    )(
-        snapshot, payoff, sensitivity, classes
-    )
+    marked = (classes + 1).astype(BF16)[None]
+    everything = jnp.concatenate([snapshot, payoff, sensitivity, marked], axis=0)
+    to_down, to_up = vmem_call(edge_kernel, (tile, tile), [pltpu.VMEM((ROWS, COLS), F32)] * 2)(everything)
     up = shift(to_down, "row", 1)
     down = shift(to_up, "row", -1)
 
     scale = jnp.broadcast_to(check_index.reshape(1, 1), (1, 64))
     layer = sd((CLASSES, 64), F32)
-    table, feature, one, two = vmem_call(
-        table_kernel, (sd((72, COLS), F32), layer, layer, layer), [pltpu.VMEM((32, COLS), F32)]
+    square = sd((64, 64), BF16)
+    table, feature, one, two, scale, w_one, w_two, w_three = vmem_call(
+        table_kernel,
+        (sd((72, COLS), F32), layer, layer, layer, sd((1, 64), jnp.int32), square, square, sd((OUTS, 64), BF16)),
+        [pltpu.VMEM((32, COLS), F32), pltpu.VMEM((CLASSES, 64), BF16), pltpu.VMEM((1, 64), BF16),
+         pltpu.SemaphoreType.DMA((6,))],
+        source=pltpu.HBM,
     )(scale, embed, time_vec.reshape(1, -1), w_one, w_two, w_three.T)
 
-    ext = pltpu.VMEM((GOALS, EXT, COLS), F32)
     plane = pltpu.VMEM((EXT, COLS), F32)
     edge = sd((OCT + 1, 32, COLS), BF16)
-    to_right, to_left = vmem_call(strip_kernel, (edge, edge), [ext, ext, ext, plane])(
-        snapshot, payoff, sensitivity, classes, up, down
-    )
+    ext = sd((GOALS, EXT, COLS), F32)
+    to_right, to_left, val, rew, sen, cls = vmem_call(
+        strip_kernel, (edge, edge, ext, ext, ext, sd((EXT, COLS), F32))
+    )(everything, up, down, table)
     left = shift(to_right, "col", 1)
     right = shift(to_left, "col", -1)
 
@@ -440,19 +461,22 @@
         return pltpu.VMEM(shape + (COLS,), F32)
 
     n = ACTIONS * POINTS
+    chance, bonus, mask, slope = vmem_call(
+        map_kernel,
+        (sd((n, EXT, COLS), F32), sd((ACTIONS, EXT, COLS), F32), sd((EXT, COLS), F32), sd((n, ROWS, COLS), F32)),
+    )(cls, table)
     snap, pay, sums = vmem_call(
         main_kernel,
         (tile, tile, sd((4, COLS), F32)),
         [
-            many(ITERS, GOALS, EXT), ext, ext, plane,
-            many(ITERS, OCT, EXT), strip, strip, plane,
-            many(n, EXT), many(n, EXT), many(ACTIONS, EXT), many(ACTIONS, EXT), plane, plane, many(n, ROWS),
+            many(ITERS - 1, GOALS, EXT), many(ITERS, OCT, EXT), strip, strip, plane,
+            many(n, EXT), many(ACTIONS, EXT), plane,
             many(ITERS, ACTIONS, GOALS, EXT), many(ITERS, ACTIONS, OCT, EXT),
             many(ITERS, GOALS, EXT), many(ITERS, GOALS, EXT),
-            many(2, POINTS, GOALS, EXT), many(2, POINTS, OCT, EXT),
+            many(2, POINTS, GOALS, EXT), many(2, POINTS, OCT, EXT), many(GOALS, EXT),
             many(OUTS, ROWS), many(GOALS, ROWS), many(GOALS, ROWS),
         ],
-    )(snapshot, payoff, sensitivity, classes, up, down, left, right, table)
+    )(val, rew, sen, cls, chance, bonus, mask, slope, left, right, table)
 
     sums = jnp.sum(spread(sums, "row"), axis=0)
     parts = spread(sums, "col")
@@ -464,7 +488,7 @@
     grads = vmem_call(
         last, (layer, sd((64,), F32), sd((64, 64), F32), sd((64, 64), F32), sd((OUTS, 64), F32)),
         [pltpu.VMEM((CLASSES, COLS), F32)],
-    )(parts, scale, feature, one, two, w_one, w_two, w_three.T)
+    )(parts, scale, feature, one, two, w_one, w_two, w_three)
     return (snap, pay, grads[0], grads[1], grads[2], grads[3], grads[4].T)
 
 

time: 81.3 us -> 77.8 us (0.957)
  local copies, waits for them, and re-layouts: 4.05 us -> 0.67 us
  other arithmetic: 0.03 us -> 1.76 us
  Pallas kernels: 13.3 us -> 12.1 us
    unnamed x22 -> x10, local copies, waits for them, and re-layouts: 4.03 us -> 0.65 us
    pallas_call x5 -> x6, Pallas kernels: 13.3 us -> 12.1 us  [vmem_call(): pl.pallas_call(kernel, out_shape=out_shape, in_specs=[given] * len(args),...]
    concatenate x0 -> x1, other arithmetic: none -> 1.03 us  [body(): jnp.concatenate([snapshot, payoff, sensitivity, marked], axis=0)]
  transfers between devices with their start and end apart: 4 -> 4, of which waited for: 3 -> 2; matrix products, arithmetic and copies ran while one was open for 0% -> 0% of each run, Pallas kernels for 1% -> 1%
where the time goes in v3:
time: 77.8 us; the launch traced here: 77.4 us
  blocking collectives  43.5 us (56%)
  starting transfers between devices  13.8 us (18%)
  Pallas kernels  12.1 us (16%)
  waiting for transfers between devices  4.22 us (5%)
  other arithmetic  1.76 us (2%)
  between operations  1.43 us (2%)
    all_to_all x2, blocking collectives, spread(): lax.all_to_all(jnp.broadcast_to(x[None], (size,) + x.shape), axis, 0, 0,...  43.5 us
    ppermute x4, starting transfers between devices, shift(): return lax.ppermute(x, axis, pairs)  13.8 us
    pallas_call x6, Pallas kernels, vmem_call(): pl.pallas_call(kernel, out_shape=out_shape, in_specs=[given] * len(args),...  12.1 us
    ppermute x4, waiting for transfers between devices, shift(): return lax.ppermute(x, axis, pairs)  4.22 us
  transfers between devices with their start and end apart: 4, of which 2 were waited for; matrix products, arithmetic and copies ran while one was open for 0% of the time, Pallas kernels for 1%

profile of v3, /device:TPU:1, one launch (start us, length us, event | category | flops | bytes accessed | tf_op | source)
XLA Modules:
  0.0 77.4 jit_solution(8190843159858407459)
XLA Ops:
  0.6 0.7 fusion
  1.3 1.0 %pad_maximum_fusion.all_ref = bf16[73,16,128]{2,1,0:T(8,128)(2,1)S(1)} fusion(bf16[1,16,128]{2,1,0:T(8,128)(2,1)S(1)} %fusion, bf16[24,16,128]{2,1,0:T(8,128)(2,1)} %param.14, bf16[24,16,128]{2,1,0:T(8,128)(2,1)} %param.13, bf16[24,16,128]{2,1,0:T(8,128)(2,1)} %param.12), kind=kLoop, calls=%fused_computation | loop fusion | flops 448512 | bytes 598016 | tf_op jit(solution)/shard_map/concatenate | solution.py:433
  2.4 0.0 copy-start
  2.4 0.0 copy-start.1
  2.4 0.2 shard_map.153
  2.6 4.0 %collective-permute-start = (bf16[24,16,128]{2,1,0:T(8,128)(2,1)S(1)}, bf16[24,16,128]{2,1,0:T(8,128)(2,1)S(1)}, u32[]{:S(2)}, u32[]{:S(2)}) collective-permute-start(bf16[24,16,128]{2,1,0:T(8,128)(2,1)S(1)} %get-tuple-element.35), channel_id=1, source_target_pairs={{0,32},{32,64},{64,96},{96,128},{128,160},{160,192},{192,224},{224... | collective-permute-start | bytes 294920 | tf_op jit(solution)/shard_map/ppermute | solution.py:421
  6.6 1.3 %collective-permute-start.1 = (bf16[24,16,128]{2,1,0:T(8,128)(2,1)S(1)}, bf16[24,16,128]{2,1,0:T(8,128)(2,1)S(1)}, u32[]{:S(2)}, u32[]{:S(2)}) collective-permute-start(bf16[24,16,128]{2,1,0:T(8,128)(2,1)S(1)} %get-tuple-element.36), channel_id=1, source_target_pairs={{32,0},{64,32},{96,64},{128,96},{160,128},{192,160},{224,192},{256... | collective-permute-start | bytes 294920 | tf_op jit(solution)/shard_map/ppermute | solution.py:421
  8.5 0.0 copy-start.3
  8.6 0.0 copy-start.4
  8.6 0.0 copy-done
  8.6 0.6 copy-done.3
  9.2 0.5 shard_map.154
  9.8 0.0 collective-permute-done.up_ref
  9.8 2.2 %collective-permute-done.1.down_ref = bf16[24,16,128]{2,1,0:T(8,128)(2,1)S(1)} collective-permute-done((bf16[24,16,128]{2,1,0:T(8,128)(2,1)S(1)}, bf16[24,16,128]{2,1,0:T(8,128)(2,1)S(1)}, u32[]{:S(2)}, u32[]{:S(2)}) %collective-permute-start.1) | collective-permute-done | bytes 98336 | tf_op jit(solution)/shard_map/ppermute | solution.py:421
  12.0 0.7 shard_map.155
  12.7 5.5 %collective-permute-start.2 = (bf16[4,32,128]{2,1,0:T(8,128)(2,1)S(1)}, bf16[4,32,128]{2,1,0:T(8,128)(2,1)S(1)}, u32[]{:S(2)}, u32[]{:S(2)}) collective-permute-start(bf16[4,32,128]{2,1,0:T(8,128)(2,1)S(1)} %get-tuple-element.46), channel_id=1, source_target_pairs={{0,1},{1,2},{2,3},{3,4},{4,5},{5,6},{6,7},{7,8},{8,9},{9,10},{10,1... | collective-permute-start | bytes 98312 | tf_op jit(solution)/shard_map/ppermute | solution.py:421
  18.2 3.0 %collective-permute-start.3 = (bf16[4,32,128]{2,1,0:T(8,128)(2,1)S(1)}, bf16[4,32,128]{2,1,0:T(8,128)(2,1)S(1)}, u32[]{:S(2)}, u32[]{:S(2)}) collective-permute-start(bf16[4,32,128]{2,1,0:T(8,128)(2,1)S(1)} %get-tuple-element.47), channel_id=1, source_target_pairs={{1,0},{2,1},{3,2},{4,3},{5,4},{6,5},{7,6},{8,7},{9,8},{10,9},{11,1... | collective-permute-start | bytes 98312 | tf_op jit(solution)/shard_map/ppermute | solution.py:421
  21.2 0.2 shard_map.156
  21.4 0.0 collective-permute-done.2.lb_ref
  21.4 2.0 %collective-permute-done.3.rb_ref = bf16[4,32,128]{2,1,0:T(8,128)(2,1)S(1)} collective-permute-done((bf16[4,32,128]{2,1,0:T(8,128)(2,1)S(1)}, bf16[4,32,128]{2,1,0:T(8,128)(2,1)S(1)}, u32[]{:S(2)}, u32[]{:S(2)}) %collective-permute-start.3) | collective-permute-done | bytes 32800 | tf_op jit(solution)/shard_map/ppermute | solution.py:421
  23.5 9.1 %shard_map.157 = (bf16[24,16,128]{2,1,0:T(8,128)(2,1)}, bf16[24,16,128]{2,1,0:T(8,128)(2,1)}, f32[4,128]{1,0:T(4,128)S(1)}) custom-call(f32[24,48,128]{2,1,0:T(8,128)S(1)} %get-tuple-element.38.val0, f32[24,48,128]{2,1,0:T(8,128)S(1)} %get-tuple-element.39.rew, f32[24,48,128]{2,1,0:T(8,128)S(1)} %get-tuple-element.40.sen, ...), custom_call_target="tpu_custom_call" | custom-call | tf_op jit(solution)/shard_map/pallas_call | solution.py:33
  32.6 14.2 %all_to_all.10 = f32[16,4,128]{2,1,0:T(4,128)S(1)} all-to-all(f32[16,4,128]{2,1,0:T(4,128)S(1)} %broadcast_in_dim.25), channel_id=1, replica_groups=mesh['row'=16,'col'=32] {'row'}, dimensions={0} | all-to-all | bytes 65536 | tf_op jit(solution)/shard_map/all_to_all | solution.py:426
  46.8 29.2 %all_to_all.11.refs_0_ = f32[32,4,128]{2,1,0:T(4,128)S(1)} all-to-all(f32[32,4,128]{2,1,0:T(4,128)S(1)} %broadcast_in_dim.26), channel_id=1, replica_groups=mesh['row'=16,'col'=32] {'col'}, dimensions={0} | all-to-all | bytes 131072 | tf_op jit(solution)/shard_map/all_to_all | solution.py:426
  76.1 1.3 %shard_map.158 = (f32[16,64]{1,0:T(8,128)}, f32[64]{0:T(128)}, f32[64,64]{1,0:T(8,128)}, f32[64,64]{1,0:T(8,128)}, f32[24,64]{1,0:T(8,128)}) custom-call(f32[32,4,128]{2,1,0:T(4,128)S(1)} %all_to_all.11.refs_0_, s32[1,64]{1,0:T(1,128)S(1)} %get-tuple-element.51.refs_1_, f32[16,64]{1,0:T(8,128)S(1)} %get-tuple-element.52.refs_2_, ...), custom_call_target="tpu_custom_call" | custom-call | tf_op jit(solution)/shard_map/pallas_call | solution.py:33
  (8 shorter events, 0.1 us)
Async XLA Ops:
  2.4 6.2 %copy-start = (bf16[64,64]{1,0:T(8,128)(2,1)S(1)}, bf16[64,64]{1,0:T(8,128)(2,1)}, u32[]{:S(2)}) copy-start(bf16[64,64]{1,0:T(8,128)(2,1)} %w1_hbm.1) | copy-start | bytes 24580
  2.4 6.2 %copy-start.1 = (bf16[64,64]{1,0:T(8,128)(2,1)S(1)}, bf16[64,64]{1,0:T(8,128)(2,1)}, u32[]{:S(2)}) copy-start(bf16[64,64]{1,0:T(8,128)(2,1)} %w2_hbm.1) | copy-start | bytes 24580
  2.5 6.1 %copy-start.2 = (bf16[64,24]{0,1:T(8,128)(2,1)S(1)}, bf16[64,24]{0,1:T(8,128)(2,1)}, u32[]{:S(2)}) copy-start(bf16[64,24]{0,1:T(8,128)(2,1)} %param.19) | copy-start | bytes 9220
  2.6 7.2 %collective-permute-start = (bf16[24,16,128]{2,1,0:T(8,128)(2,1)S(1)}, bf16[24,16,128]{2,1,0:T(8,128)(2,1)S(1)}, u32[]{:S(2)}, u32[]{:S(2)}) collective-permute-start(bf16[24,16,128]{2,1,0:T(8,128)(2,1)S(1)} %get-tuple-element.35), channel_id=1, source_target_pairs={{0,32},{32,64},{64,96},{96,128},{128,160},{160,192},{192,224},{224... | collective-permute-start | bytes 294920 | tf_op jit(solution)/shard_map/ppermute | solution.py:421
  6.6 5.4 %collective-permute-start.1 = (bf16[24,16,128]{2,1,0:T(8,128)(2,1)S(1)}, bf16[24,16,128]{2,1,0:T(8,128)(2,1)S(1)}, u32[]{:S(2)}, u32[]{:S(2)}) collective-permute-start(bf16[24,16,128]{2,1,0:T(8,128)(2,1)S(1)} %get-tuple-element.36), channel_id=1, source_target_pairs={{32,0},{64,32},{96,64},{128,96},{160,128},{192,160},{224,192},{256... | collective-permute-start | bytes 294920 | tf_op jit(solution)/shard_map/ppermute | solution.py:421
  8.5 0.7 copy-start.3
  8.6 0.7 copy-start.4
  12.7 8.7 %collective-permute-start.2 = (bf16[4,32,128]{2,1,0:T(8,128)(2,1)S(1)}, bf16[4,32,128]{2,1,0:T(8,128)(2,1)S(1)}, u32[]{:S(2)}, u32[]{:S(2)}) collective-permute-start(bf16[4,32,128]{2,1,0:T(8,128)(2,1)S(1)} %get-tuple-element.46), channel_id=1, source_target_pairs={{0,1},{1,2},{2,3},{3,4},{4,5},{5,6},{6,7},{7,8},{8,9},{9,10},{10,1... | collective-permute-start | bytes 98312 | tf_op jit(solution)/shard_map/ppermute | solution.py:421
  18.2 5.2 %collective-permute-start.3 = (bf16[4,32,128]{2,1,0:T(8,128)(2,1)S(1)}, bf16[4,32,128]{2,1,0:T(8,128)(2,1)S(1)}, u32[]{:S(2)}, u32[]{:S(2)}) collective-permute-start(bf16[4,32,128]{2,1,0:T(8,128)(2,1)S(1)} %get-tuple-element.47), channel_id=1, source_target_pairs={{1,0},{2,1},{3,2},{4,3},{5,4},{6,5},{7,6},{8,7},{9,8},{10,9},{11,1... | collective-permute-start | bytes 98312 | tf_op jit(solution)/shard_map/ppermute | solution.py:421

commit v4 on v3

--- a/solution.py
+++ b/solution.py
@@ -421,9 +421,10 @@
     return lax.ppermute(x, axis, pairs)
 
 
-def spread(x, axis):
-    size = lax.axis_size(axis)
-    return lax.all_to_all(jnp.broadcast_to(x[None], (size,) + x.shape), axis, 0, 0, tiled=True)
+def spread(x, axis, groups=None):
+    size = lax.axis_size(axis) if groups is None else len(groups[0])
+    copies = jnp.broadcast_to(x[None], (size,) + x.shape)
+    return lax.all_to_all(copies, axis, 0, 0, tiled=True, axis_index_groups=groups)
 
 
 def body(classes, check_index, snapshot, payoff, sensitivity, embed, time_vec, w_one, w_two, w_three):
@@ -478,8 +479,11 @@
         ],
     )(val, rew, sen, cls, chance, bonus, mask, slope, left, right, table)
 
-    sums = jnp.sum(spread(sums, "row"), axis=0)
-    parts = spread(sums, "col")
+    rows, cols = lax.axis_size("row"), lax.axis_size("col")
+    near = [[r * cols + c + i for r in range(rows) for i in range(2)] for c in range(0, cols, 2)]
+    along = [list(range(i, cols, 2)) for i in range(2)]
+    sums = jnp.sum(spread(sums, ("row", "col"), near), axis=0)
+    parts = spread(sums, "col", along)
     factor = 1.0 / math.sqrt(ROWS * lax.axis_size("row") * COLS * lax.axis_size("col"))
 
     def last(*refs):

time: 77.8 us -> 76 us (0.977)
  blocking collectives: 43.5 us -> 41.6 us
    all_to_all x2, blocking collectives: 43.5 us -> 41.6 us  [spread(): lax.all_to_all(copies, axis, 0, 0, tiled=True, axis_index_groups=groups)]
where the time goes in v4:
time: 76 us; the launch traced here: 75.6 us
  blocking collectives  41.6 us (55%)
  starting transfers between devices  13.8 us (18%)
  Pallas kernels  12.1 us (16%)
  waiting for transfers between devices  4.22 us (6%)
  other arithmetic  1.78 us (2%)
  between operations  1.43 us (2%)
    all_to_all x2, blocking collectives, spread(): lax.all_to_all(copies, axis, 0, 0, tiled=True, axis_index_groups=groups)  41.6 us
    ppermute x4, starting transfers between devices, shift(): return lax.ppermute(x, axis, pairs)  13.8 us
    pallas_call x6, Pallas kernels, vmem_call(): pl.pallas_call(kernel, out_shape=out_shape, in_specs=[given] * len(args),...  12.1 us
    ppermute x4, waiting for transfers between devices, shift(): return lax.ppermute(x, axis, pairs)  4.22 us
  transfers between devices with their start and end apart: 4, of which 2 were waited for; matrix products, arithmetic and copies ran while one was open for 0% of the time, Pallas kernels for 1%

profile of v4, /device:TPU:1, one launch (start us, length us, event | category | flops | bytes accessed | tf_op | source)
XLA Modules:
  0.0 75.6 jit_solution(8131631495335818965)
XLA Ops:
  0.6 0.7 fusion
  1.3 1.0 %pad_maximum_fusion.all_ref = bf16[73,16,128]{2,1,0:T(8,128)(2,1)S(1)} fusion(bf16[1,16,128]{2,1,0:T(8,128)(2,1)S(1)} %fusion, bf16[24,16,128]{2,1,0:T(8,128)(2,1)} %param.14, bf16[24,16,128]{2,1,0:T(8,128)(2,1)} %param.13, bf16[24,16,128]{2,1,0:T(8,128)(2,1)} %param.12), kind=kLoop, calls=%fused_computation | loop fusion | flops 448512 | bytes 598016 | tf_op jit(solution)/shard_map/concatenate | solution.py:434
  2.4 0.0 copy-start
  2.4 0.0 copy-start.1
  2.4 0.2 shard_map.153
  2.6 4.0 %collective-permute-start = (bf16[24,16,128]{2,1,0:T(8,128)(2,1)S(1)}, bf16[24,16,128]{2,1,0:T(8,128)(2,1)S(1)}, u32[]{:S(2)}, u32[]{:S(2)}) collective-permute-start(bf16[24,16,128]{2,1,0:T(8,128)(2,1)S(1)} %get-tuple-element.35), channel_id=1, source_target_pairs={{0,32},{32,64},{64,96},{96,128},{128,160},{160,192},{192,224},{224... | collective-permute-start | bytes 294920 | tf_op jit(solution)/shard_map/ppermute | solution.py:421
  6.6 1.3 %collective-permute-start.1 = (bf16[24,16,128]{2,1,0:T(8,128)(2,1)S(1)}, bf16[24,16,128]{2,1,0:T(8,128)(2,1)S(1)}, u32[]{:S(2)}, u32[]{:S(2)}) collective-permute-start(bf16[24,16,128]{2,1,0:T(8,128)(2,1)S(1)} %get-tuple-element.36), channel_id=1, source_target_pairs={{32,0},{64,32},{96,64},{128,96},{160,128},{192,160},{224,192},{256... | collective-permute-start | bytes 294920 | tf_op jit(solution)/shard_map/ppermute | solution.py:421
  8.5 0.0 copy-start.3
  8.6 0.0 copy-start.4
  8.6 0.0 copy-done
  8.6 0.6 copy-done.3
  9.2 0.5 shard_map.154
  9.8 0.0 collective-permute-done.up_ref
  9.8 2.2 %collective-permute-done.1.down_ref = bf16[24,16,128]{2,1,0:T(8,128)(2,1)S(1)} collective-permute-done((bf16[24,16,128]{2,1,0:T(8,128)(2,1)S(1)}, bf16[24,16,128]{2,1,0:T(8,128)(2,1)S(1)}, u32[]{:S(2)}, u32[]{:S(2)}) %collective-permute-start.1) | collective-permute-done | bytes 98336 | tf_op jit(solution)/shard_map/ppermute | solution.py:421
  12.0 0.7 shard_map.155
  12.7 5.5 %collective-permute-start.2 = (bf16[4,32,128]{2,1,0:T(8,128)(2,1)S(1)}, bf16[4,32,128]{2,1,0:T(8,128)(2,1)S(1)}, u32[]{:S(2)}, u32[]{:S(2)}) collective-permute-start(bf16[4,32,128]{2,1,0:T(8,128)(2,1)S(1)} %get-tuple-element.46), channel_id=1, source_target_pairs={{0,1},{1,2},{2,3},{3,4},{4,5},{5,6},{6,7},{7,8},{8,9},{9,10},{10,1... | collective-permute-start | bytes 98312 | tf_op jit(solution)/shard_map/ppermute | solution.py:421
  18.2 3.0 %collective-permute-start.3 = (bf16[4,32,128]{2,1,0:T(8,128)(2,1)S(1)}, bf16[4,32,128]{2,1,0:T(8,128)(2,1)S(1)}, u32[]{:S(2)}, u32[]{:S(2)}) collective-permute-start(bf16[4,32,128]{2,1,0:T(8,128)(2,1)S(1)} %get-tuple-element.47), channel_id=1, source_target_pairs={{1,0},{2,1},{3,2},{4,3},{5,4},{6,5},{7,6},{8,7},{9,8},{10,9},{11,1... | collective-permute-start | bytes 98312 | tf_op jit(solution)/shard_map/ppermute | solution.py:421
  21.2 0.2 shard_map.156
  21.4 0.0 collective-permute-done.2.lb_ref
  21.4 2.0 %collective-permute-done.3.rb_ref = bf16[4,32,128]{2,1,0:T(8,128)(2,1)S(1)} collective-permute-done((bf16[4,32,128]{2,1,0:T(8,128)(2,1)S(1)}, bf16[4,32,128]{2,1,0:T(8,128)(2,1)S(1)}, u32[]{:S(2)}, u32[]{:S(2)}) %collective-permute-start.3) | collective-permute-done | bytes 32800 | tf_op jit(solution)/shard_map/ppermute | solution.py:421
  23.5 9.1 %shard_map.157 = (bf16[24,16,128]{2,1,0:T(8,128)(2,1)}, bf16[24,16,128]{2,1,0:T(8,128)(2,1)}, f32[4,128]{1,0:T(4,128)S(1)}) custom-call(f32[24,48,128]{2,1,0:T(8,128)S(1)} %get-tuple-element.38.val0, f32[24,48,128]{2,1,0:T(8,128)S(1)} %get-tuple-element.39.rew, f32[24,48,128]{2,1,0:T(8,128)S(1)} %get-tuple-element.40.sen, ...), custom_call_target="tpu_custom_call" | custom-call | tf_op jit(solution)/shard_map/pallas_call | solution.py:33
  32.6 15.6 %all_to_all.10 = f32[32,4,128]{2,1,0:T(4,128)S(1)} all-to-all(f32[32,4,128]{2,1,0:T(4,128)S(1)} %broadcast_in_dim.25), channel_id=1, replica_groups={{0,1,32,33,64,65,96,97,128,129,160,161,192,193,224,225,256,257,288,289,..., dimensions={0} | all-to-all | bytes 131072 | tf_op jit(solution)/shard_map/all_to_all | solution.py:427
  48.2 26.0 %all_to_all.11.refs_0_ = f32[16,4,128]{2,1,0:T(4,128)S(1)} all-to-all(f32[16,4,128]{2,1,0:T(4,128)S(1)} %broadcast_in_dim.26), channel_id=1, replica_groups={{0,2,4,6,8,10,12,14,16,18,20,22,24,26,28,30},{1,3,5,7,9,11,13,15,17,19,..., dimensions={0} | all-to-all | bytes 65536 | tf_op jit(solution)/shard_map/all_to_all | solution.py:427
  74.3 1.3 %shard_map.158 = (f32[16,64]{1,0:T(8,128)}, f32[64]{0:T(128)}, f32[64,64]{1,0:T(8,128)}, f32[64,64]{1,0:T(8,128)}, f32[24,64]{1,0:T(8,128)}) custom-call(f32[16,4,128]{2,1,0:T(4,128)S(1)} %all_to_all.11.refs_0_, s32[1,64]{1,0:T(1,128)S(1)} %get-tuple-element.51.refs_1_, f32[16,64]{1,0:T(8,128)S(1)} %get-tuple-element.52.refs_2_, ...), custom_call_target="tpu_custom_call" | custom-call | tf_op jit(solution)/shard_map/pallas_call | solution.py:33
  (8 shorter events, 0.1 us)
Async XLA Ops:
  2.4 6.2 %copy-start = (bf16[64,64]{1,0:T(8,128)(2,1)S(1)}, bf16[64,64]{1,0:T(8,128)(2,1)}, u32[]{:S(2)}) copy-start(bf16[64,64]{1,0:T(8,128)(2,1)} %w1_hbm.1) | copy-start | bytes 24580
  2.4 6.2 %copy-start.1 = (bf16[64,64]{1,0:T(8,128)(2,1)S(1)}, bf16[64,64]{1,0:T(8,128)(2,1)}, u32[]{:S(2)}) copy-start(bf16[64,64]{1,0:T(8,128)(2,1)} %w2_hbm.1) | copy-start | bytes 24580
  2.5 6.1 %copy-start.2 = (bf16[64,24]{0,1:T(8,128)(2,1)S(1)}, bf16[64,24]{0,1:T(8,128)(2,1)}, u32[]{:S(2)}) copy-start(bf16[64,24]{0,1:T(8,128)(2,1)} %param.19) | copy-start | bytes 9220
  2.6 7.2 %collective-permute-start = (bf16[24,16,128]{2,1,0:T(8,128)(2,1)S(1)}, bf16[24,16,128]{2,1,0:T(8,128)(2,1)S(1)}, u32[]{:S(2)}, u32[]{:S(2)}) collective-permute-start(bf16[24,16,128]{2,1,0:T(8,128)(2,1)S(1)} %get-tuple-element.35), channel_id=1, source_target_pairs={{0,32},{32,64},{64,96},{96,128},{128,160},{160,192},{192,224},{224... | collective-permute-start | bytes 294920 | tf_op jit(solution)/shard_map/ppermute | solution.py:421
  6.6 5.4 %collective-permute-start.1 = (bf16[24,16,128]{2,1,0:T(8,128)(2,1)S(1)}, bf16[24,16,128]{2,1,0:T(8,128)(2,1)S(1)}, u32[]{:S(2)}, u32[]{:S(2)}) collective-permute-start(bf16[24,16,128]{2,1,0:T(8,128)(2,1)S(1)} %get-tuple-element.36), channel_id=1, source_target_pairs={{32,0},{64,32},{96,64},{128,96},{160,128},{192,160},{224,192},{256... | collective-permute-start | bytes 294920 | tf_op jit(solution)/shard_map/ppermute | solution.py:421
  8.5 0.7 copy-start.3
  8.6 0.7 copy-start.4
  12.7 8.7 %collective-permute-start.2 = (bf16[4,32,128]{2,1,0:T(8,128)(2,1)S(1)}, bf16[4,32,128]{2,1,0:T(8,128)(2,1)S(1)}, u32[]{:S(2)}, u32[]{:S(2)}) collective-permute-start(bf16[4,32,128]{2,1,0:T(8,128)(2,1)S(1)} %get-tuple-element.46), channel_id=1, source_target_pairs={{0,1},{1,2},{2,3},{3,4},{4,5},{5,6},{6,7},{7,8},{8,9},{9,10},{10,1... | collective-permute-start | bytes 98312 | tf_op jit(solution)/shard_map/ppermute | solution.py:421
  18.2 5.2 %collective-permute-start.3 = (bf16[4,32,128]{2,1,0:T(8,128)(2,1)S(1)}, bf16[4,32,128]{2,1,0:T(8,128)(2,1)S(1)}, u32[]{:S(2)}, u32[]{:S(2)}) collective-permute-start(bf16[4,32,128]{2,1,0:T(8,128)(2,1)S(1)} %get-tuple-element.47), channel_id=1, source_target_pairs={{1,0},{2,1},{3,2},{4,3},{5,4},{6,5},{7,6},{8,7},{9,8},{10,9},{11,1... | collective-permute-start | bytes 98312 | tf_op jit(solution)/shard_map/ppermute | solution.py:421

commit v5 on v4

--- a/solution.py
+++ b/solution.py
@@ -482,8 +482,8 @@
     rows, cols = lax.axis_size("row"), lax.axis_size("col")
     near = [[r * cols + c + i for r in range(rows) for i in range(2)] for c in range(0, cols, 2)]
     along = [list(range(i, cols, 2)) for i in range(2)]
-    sums = jnp.sum(spread(sums, ("row", "col"), near), axis=0)
-    parts = spread(sums, "col", along)
+    sums = jnp.sum(spread(sums, "col", along), axis=0)
+    parts = spread(sums, ("row", "col"), near)
     factor = 1.0 / math.sqrt(ROWS * lax.axis_size("row") * COLS * lax.axis_size("col"))
 
     def last(*refs):

time: 76 us -> 77.3 us (1.017)
  blocking collectives: 41.6 us -> 42.9 us
    all_to_all x2, blocking collectives: 41.6 us -> 42.9 us  [spread(): lax.all_to_all(copies, axis, 0, 0, tiled=True, axis_index_groups=groups)]
where the time goes in v5:
time: 77.3 us; the launch traced here: 76.9 us
  blocking collectives  42.9 us (55%)
  starting transfers between devices  13.8 us (18%)
  Pallas kernels  12.1 us (16%)
  waiting for transfers between devices  4.22 us (5%)
  other arithmetic  1.76 us (2%)
  between operations  1.43 us (2%)
    all_to_all x2, blocking collectives, spread(): lax.all_to_all(copies, axis, 0, 0, tiled=True, axis_index_groups=groups)  42.9 us
    ppermute x4, starting transfers between devices, shift(): return lax.ppermute(x, axis, pairs)  13.8 us
    pallas_call x6, Pallas kernels, vmem_call(): pl.pallas_call(kernel, out_shape=out_shape, in_specs=[given] * len(args),...  12.1 us
    ppermute x4, waiting for transfers between devices, shift(): return lax.ppermute(x, axis, pairs)  4.22 us
  transfers between devices with their start and end apart: 4, of which 2 were waited for; matrix products, arithmetic and copies ran while one was open for 0% of the time, Pallas kernels for 1%

profile of v5, /device:TPU:1, one launch (start us, length us, event | category | flops | bytes accessed | tf_op | source)
XLA Modules:
  0.0 76.9 jit_solution(2281129898858679116)
XLA Ops:
  0.6 0.7 fusion
  1.3 1.0 %pad_maximum_fusion.all_ref = bf16[73,16,128]{2,1,0:T(8,128)(2,1)S(1)} fusion(bf16[1,16,128]{2,1,0:T(8,128)(2,1)S(1)} %fusion, bf16[24,16,128]{2,1,0:T(8,128)(2,1)} %param.14, bf16[24,16,128]{2,1,0:T(8,128)(2,1)} %param.13, bf16[24,16,128]{2,1,0:T(8,128)(2,1)} %param.12), kind=kLoop, calls=%fused_computation | loop fusion | flops 448512 | bytes 598016 | tf_op jit(solution)/shard_map/concatenate | solution.py:434
  2.4 0.0 copy-start
  2.4 0.0 copy-start.1
  2.4 0.2 shard_map.153
  2.6 4.0 %collective-permute-start = (bf16[24,16,128]{2,1,0:T(8,128)(2,1)S(1)}, bf16[24,16,128]{2,1,0:T(8,128)(2,1)S(1)}, u32[]{:S(2)}, u32[]{:S(2)}) collective-permute-start(bf16[24,16,128]{2,1,0:T(8,128)(2,1)S(1)} %get-tuple-element.35), channel_id=1, source_target_pairs={{0,32},{32,64},{64,96},{96,128},{128,160},{160,192},{192,224},{224... | collective-permute-start | bytes 294920 | tf_op jit(solution)/shard_map/ppermute | solution.py:421
  6.6 1.3 %collective-permute-start.1 = (bf16[24,16,128]{2,1,0:T(8,128)(2,1)S(1)}, bf16[24,16,128]{2,1,0:T(8,128)(2,1)S(1)}, u32[]{:S(2)}, u32[]{:S(2)}) collective-permute-start(bf16[24,16,128]{2,1,0:T(8,128)(2,1)S(1)} %get-tuple-element.36), channel_id=1, source_target_pairs={{32,0},{64,32},{96,64},{128,96},{160,128},{192,160},{224,192},{256... | collective-permute-start | bytes 294920 | tf_op jit(solution)/shard_map/ppermute | solution.py:421
  8.5 0.0 copy-start.3
  8.6 0.0 copy-start.4
  8.6 0.0 copy-done
  8.6 0.6 copy-done.3
  9.2 0.5 shard_map.154
  9.8 0.0 collective-permute-done.up_ref
  9.8 2.2 %collective-permute-done.1.down_ref = bf16[24,16,128]{2,1,0:T(8,128)(2,1)S(1)} collective-permute-done((bf16[24,16,128]{2,1,0:T(8,128)(2,1)S(1)}, bf16[24,16,128]{2,1,0:T(8,128)(2,1)S(1)}, u32[]{:S(2)}, u32[]{:S(2)}) %collective-permute-start.1) | collective-permute-done | bytes 98336 | tf_op jit(solution)/shard_map/ppermute | solution.py:421
  12.0 0.7 shard_map.155
  12.7 5.5 %collective-permute-start.2 = (bf16[4,32,128]{2,1,0:T(8,128)(2,1)S(1)}, bf16[4,32,128]{2,1,0:T(8,128)(2,1)S(1)}, u32[]{:S(2)}, u32[]{:S(2)}) collective-permute-start(bf16[4,32,128]{2,1,0:T(8,128)(2,1)S(1)} %get-tuple-element.46), channel_id=1, source_target_pairs={{0,1},{1,2},{2,3},{3,4},{4,5},{5,6},{6,7},{7,8},{8,9},{9,10},{10,1... | collective-permute-start | bytes 98312 | tf_op jit(solution)/shard_map/ppermute | solution.py:421
  18.2 3.0 %collective-permute-start.3 = (bf16[4,32,128]{2,1,0:T(8,128)(2,1)S(1)}, bf16[4,32,128]{2,1,0:T(8,128)(2,1)S(1)}, u32[]{:S(2)}, u32[]{:S(2)}) collective-permute-start(bf16[4,32,128]{2,1,0:T(8,128)(2,1)S(1)} %get-tuple-element.47), channel_id=1, source_target_pairs={{1,0},{2,1},{3,2},{4,3},{5,4},{6,5},{7,6},{8,7},{9,8},{10,9},{11,1... | collective-permute-start | bytes 98312 | tf_op jit(solution)/shard_map/ppermute | solution.py:421
  21.2 0.2 shard_map.156
  21.4 0.0 collective-permute-done.2.lb_ref
  21.4 2.0 %collective-permute-done.3.rb_ref = bf16[4,32,128]{2,1,0:T(8,128)(2,1)S(1)} collective-permute-done((bf16[4,32,128]{2,1,0:T(8,128)(2,1)S(1)}, bf16[4,32,128]{2,1,0:T(8,128)(2,1)S(1)}, u32[]{:S(2)}, u32[]{:S(2)}) %collective-permute-start.3) | collective-permute-done | bytes 32800 | tf_op jit(solution)/shard_map/ppermute | solution.py:421
  23.5 9.1 %shard_map.157 = (bf16[24,16,128]{2,1,0:T(8,128)(2,1)}, bf16[24,16,128]{2,1,0:T(8,128)(2,1)}, f32[4,128]{1,0:T(4,128)S(1)}) custom-call(f32[24,48,128]{2,1,0:T(8,128)S(1)} %get-tuple-element.38.val0, f32[24,48,128]{2,1,0:T(8,128)S(1)} %get-tuple-element.39.rew, f32[24,48,128]{2,1,0:T(8,128)S(1)} %get-tuple-element.40.sen, ...), custom_call_target="tpu_custom_call" | custom-call | tf_op jit(solution)/shard_map/pallas_call | solution.py:33
  32.6 25.9 %all_to_all.10 = f32[16,4,128]{2,1,0:T(4,128)S(1)} all-to-all(f32[16,4,128]{2,1,0:T(4,128)S(1)} %broadcast_in_dim.25), channel_id=1, replica_groups={{0,2,4,6,8,10,12,14,16,18,20,22,24,26,28,30},{1,3,5,7,9,11,13,15,17,19,..., dimensions={0} | all-to-all | bytes 65536 | tf_op jit(solution)/shard_map/all_to_all | solution.py:427
  58.5 17.0 %all_to_all.11.refs_0_ = f32[32,4,128]{2,1,0:T(4,128)S(1)} all-to-all(f32[32,4,128]{2,1,0:T(4,128)S(1)} %broadcast_in_dim.26), channel_id=1, replica_groups={{0,1,32,33,64,65,96,97,128,129,160,161,192,193,224,225,256,257,288,289,..., dimensions={0} | all-to-all | bytes 131072 | tf_op jit(solution)/shard_map/all_to_all | solution.py:427
  75.5 1.3 %shard_map.158 = (f32[16,64]{1,0:T(8,128)}, f32[64]{0:T(128)}, f32[64,64]{1,0:T(8,128)}, f32[64,64]{1,0:T(8,128)}, f32[24,64]{1,0:T(8,128)}) custom-call(f32[32,4,128]{2,1,0:T(4,128)S(1)} %all_to_all.11.refs_0_, s32[1,64]{1,0:T(1,128)S(1)} %get-tuple-element.51.refs_1_, f32[16,64]{1,0:T(8,128)S(1)} %get-tuple-element.52.refs_2_, ...), custom_call_target="tpu_custom_call" | custom-call | tf_op jit(solution)/shard_map/pallas_call | solution.py:33
  (8 shorter events, 0.1 us)
Async XLA Ops:
  2.4 6.2 %copy-start = (bf16[64,64]{1,0:T(8,128)(2,1)S(1)}, bf16[64,64]{1,0:T(8,128)(2,1)}, u32[]{:S(2)}) copy-start(bf16[64,64]{1,0:T(8,128)(2,1)} %w1_hbm.1) | copy-start | bytes 24580
  2.4 6.2 %copy-start.1 = (bf16[64,64]{1,0:T(8,128)(2,1)S(1)}, bf16[64,64]{1,0:T(8,128)(2,1)}, u32[]{:S(2)}) copy-start(bf16[64,64]{1,0:T(8,128)(2,1)} %w2_hbm.1) | copy-start | bytes 24580
  2.5 6.1 %copy-start.2 = (bf16[64,24]{0,1:T(8,128)(2,1)S(1)}, bf16[64,24]{0,1:T(8,128)(2,1)}, u32[]{:S(2)}) copy-start(bf16[64,24]{0,1:T(8,128)(2,1)} %param.19) | copy-start | bytes 9220
  2.6 7.2 %collective-permute-start = (bf16[24,16,128]{2,1,0:T(8,128)(2,1)S(1)}, bf16[24,16,128]{2,1,0:T(8,128)(2,1)S(1)}, u32[]{:S(2)}, u32[]{:S(2)}) collective-permute-start(bf16[24,16,128]{2,1,0:T(8,128)(2,1)S(1)} %get-tuple-element.35), channel_id=1, source_target_pairs={{0,32},{32,64},{64,96},{96,128},{128,160},{160,192},{192,224},{224... | collective-permute-start | bytes 294920 | tf_op jit(solution)/shard_map/ppermute | solution.py:421
  6.6 5.4 %collective-permute-start.1 = (bf16[24,16,128]{2,1,0:T(8,128)(2,1)S(1)}, bf16[24,16,128]{2,1,0:T(8,128)(2,1)S(1)}, u32[]{:S(2)}, u32[]{:S(2)}) collective-permute-start(bf16[24,16,128]{2,1,0:T(8,128)(2,1)S(1)} %get-tuple-element.36), channel_id=1, source_target_pairs={{32,0},{64,32},{96,64},{128,96},{160,128},{192,160},{224,192},{256... | collective-permute-start | bytes 294920 | tf_op jit(solution)/shard_map/ppermute | solution.py:421
  8.5 0.7 copy-start.3
  8.6 0.7 copy-start.4
  12.7 8.7 %collective-permute-start.2 = (bf16[4,32,128]{2,1,0:T(8,128)(2,1)S(1)}, bf16[4,32,128]{2,1,0:T(8,128)(2,1)S(1)}, u32[]{:S(2)}, u32[]{:S(2)}) collective-permute-start(bf16[4,32,128]{2,1,0:T(8,128)(2,1)S(1)} %get-tuple-element.46), channel_id=1, source_target_pairs={{0,1},{1,2},{2,3},{3,4},{4,5},{5,6},{6,7},{7,8},{8,9},{9,10},{10,1... | collective-permute-start | bytes 98312 | tf_op jit(solution)/shard_map/ppermute | solution.py:421
  18.2 5.2 %collective-permute-start.3 = (bf16[4,32,128]{2,1,0:T(8,128)(2,1)S(1)}, bf16[4,32,128]{2,1,0:T(8,128)(2,1)S(1)}, u32[]{:S(2)}, u32[]{:S(2)}) collective-permute-start(bf16[4,32,128]{2,1,0:T(8,128)(2,1)S(1)} %get-tuple-element.47), channel_id=1, source_target_pairs={{1,0},{2,1},{3,2},{4,3},{5,4},{6,5},{7,6},{8,7},{9,8},{10,9},{11,1... | collective-permute-start | bytes 98312 | tf_op jit(solution)/shard_map/ppermute | solution.py:421

commit v6 on v4

--- a/solution.py
+++ b/solution.py
@@ -59,6 +59,16 @@
 
 def dot(a, b, dims, precision=None):
     return lax.dot_general(a, b, (dims, ((), ())), precision=precision, preferred_element_type=F32)
+
+
+def split_dot(x, y, dims):
+    total = None
+    for _ in range(3):
+        part = x.astype(BF16)
+        x = x - part.astype(F32)
+        one = dot(part, y, dims)
+        total = one if total is None else total + one
+    return total
 
 
 def table_kernel(scale_hbm, embed_hbm, time_hbm, w1_hbm, w2_hbm, w3_hbm, tab_ref, f_ref, h1_ref, h2_ref,
@@ -404,10 +414,10 @@
         classed[4 * q : 4 * q + 4, :] = turn(total, -32 * q)
     sums = classed[:, 0:OUTS]
     f, h1, h2 = f_ref[...], h1_ref[...], h2_ref[...]
-    two_grad = dot(sums, w3_ref[...].astype(F32), ((1,), (0,)), HIGHEST) * (1.0 - h2 * h2)
-    one_grad = dot(two_grad, w2_ref[...].astype(F32), ((1,), (1,)), HIGHEST) * (1.0 - h1 * h1)
-    feature_grad = dot(one_grad, w1_ref[...].astype(F32), ((1,), (1,)), HIGHEST)
-    three_ref[...] = dot(sums, h2, ((0,), (0,)), HIGHEST)
+    two_grad = split_dot(sums, w3_ref[...], ((1,), (0,))) * (1.0 - h2 * h2)
+    one_grad = split_dot(two_grad, w2_ref[...], ((1,), (1,))) * (1.0 - h1 * h1)
+    feature_grad = split_dot(one_grad, w1_ref[...], ((1,), (1,)))
+    three_ref[...] = split_dot(sums, h2.astype(BF16), ((0,), (0,)))
     two_ref[...] = dot(h1, two_grad, ((0,), (0,)), HIGHEST)
     one_ref[...] = dot(f, one_grad, ((0,), (0,)), HIGHEST)
     embed_ref[...] = feature_grad

time: 76 us -> 75.9 us (level)
  no operation moved by 1% of the time
where the time goes in v6:
time: 75.9 us; the launch traced here: 75.5 us
  blocking collectives  41.6 us (55%)
  starting transfers between devices  13.8 us (18%)
  Pallas kernels  11.9 us (16%)
  waiting for transfers between devices  4.22 us (6%)
  other arithmetic  1.78 us (2%)
  between operations  1.43 us (2%)
    all_to_all x2, blocking collectives, spread(): lax.all_to_all(copies, axis, 0, 0, tiled=True, axis_index_groups=groups)  41.6 us
    ppermute x4, starting transfers between devices, shift(): return lax.ppermute(x, axis, pairs)  13.8 us
    pallas_call x6, Pallas kernels, vmem_call(): pl.pallas_call(kernel, out_shape=out_shape, in_specs=[given] * len(args),...  11.9 us
    ppermute x4, waiting for transfers between devices, shift(): return lax.ppermute(x, axis, pairs)  4.22 us
  transfers between devices with their start and end apart: 4, of which 2 were waited for; matrix products, arithmetic and copies ran while one was open for 0% of the time, Pallas kernels for 1%

profile of v6, /device:TPU:1, one launch (start us, length us, event | category | flops | bytes accessed | tf_op | source)
XLA Modules:
  0.0 75.5 jit_solution(7852308318764505434)
XLA Ops:
  0.6 0.7 fusion
  1.3 1.0 %pad_maximum_fusion.all_ref = bf16[73,16,128]{2,1,0:T(8,128)(2,1)S(1)} fusion(bf16[1,16,128]{2,1,0:T(8,128)(2,1)S(1)} %fusion, bf16[24,16,128]{2,1,0:T(8,128)(2,1)} %param.14, bf16[24,16,128]{2,1,0:T(8,128)(2,1)} %param.13, bf16[24,16,128]{2,1,0:T(8,128)(2,1)} %param.12), kind=kLoop, calls=%fused_computation | loop fusion | flops 448512 | bytes 598016 | tf_op jit(solution)/shard_map/concatenate | solution.py:444
  2.4 0.0 copy-start
  2.4 0.0 copy-start.1
  2.4 0.2 shard_map.153
  2.6 4.0 %collective-permute-start = (bf16[24,16,128]{2,1,0:T(8,128)(2,1)S(1)}, bf16[24,16,128]{2,1,0:T(8,128)(2,1)S(1)}, u32[]{:S(2)}, u32[]{:S(2)}) collective-permute-start(bf16[24,16,128]{2,1,0:T(8,128)(2,1)S(1)} %get-tuple-element.35), channel_id=1, source_target_pairs={{0,32},{32,64},{64,96},{96,128},{128,160},{160,192},{192,224},{224... | collective-permute-start | bytes 294920 | tf_op jit(solution)/shard_map/ppermute | solution.py:431
  6.6 1.3 %collective-permute-start.1 = (bf16[24,16,128]{2,1,0:T(8,128)(2,1)S(1)}, bf16[24,16,128]{2,1,0:T(8,128)(2,1)S(1)}, u32[]{:S(2)}, u32[]{:S(2)}) collective-permute-start(bf16[24,16,128]{2,1,0:T(8,128)(2,1)S(1)} %get-tuple-element.36), channel_id=1, source_target_pairs={{32,0},{64,32},{96,64},{128,96},{160,128},{192,160},{224,192},{256... | collective-permute-start | bytes 294920 | tf_op jit(solution)/shard_map/ppermute | solution.py:431
  8.5 0.0 copy-start.3
  8.6 0.0 copy-start.4
  8.6 0.0 copy-done
  8.6 0.6 copy-done.3
  9.2 0.5 shard_map.154
  9.8 0.0 collective-permute-done.up_ref
  9.8 2.2 %collective-permute-done.1.down_ref = bf16[24,16,128]{2,1,0:T(8,128)(2,1)S(1)} collective-permute-done((bf16[24,16,128]{2,1,0:T(8,128)(2,1)S(1)}, bf16[24,16,128]{2,1,0:T(8,128)(2,1)S(1)}, u32[]{:S(2)}, u32[]{:S(2)}) %collective-permute-start.1) | collective-permute-done | bytes 98336 | tf_op jit(solution)/shard_map/ppermute | solution.py:431
  12.0 0.7 shard_map.155
  12.7 5.5 %collective-permute-start.2 = (bf16[4,32,128]{2,1,0:T(8,128)(2,1)S(1)}, bf16[4,32,128]{2,1,0:T(8,128)(2,1)S(1)}, u32[]{:S(2)}, u32[]{:S(2)}) collective-permute-start(bf16[4,32,128]{2,1,0:T(8,128)(2,1)S(1)} %get-tuple-element.46), channel_id=1, source_target_pairs={{0,1},{1,2},{2,3},{3,4},{4,5},{5,6},{6,7},{7,8},{8,9},{9,10},{10,1... | collective-permute-start | bytes 98312 | tf_op jit(solution)/shard_map/ppermute | solution.py:431
  18.2 3.0 %collective-permute-start.3 = (bf16[4,32,128]{2,1,0:T(8,128)(2,1)S(1)}, bf16[4,32,128]{2,1,0:T(8,128)(2,1)S(1)}, u32[]{:S(2)}, u32[]{:S(2)}) collective-permute-start(bf16[4,32,128]{2,1,0:T(8,128)(2,1)S(1)} %get-tuple-element.47), channel_id=1, source_target_pairs={{1,0},{2,1},{3,2},{4,3},{5,4},{6,5},{7,6},{8,7},{9,8},{10,9},{11,1... | collective-permute-start | bytes 98312 | tf_op jit(solution)/shard_map/ppermute | solution.py:431
  21.2 0.2 shard_map.156
  21.4 0.0 collective-permute-done.2.lb_ref
  21.4 2.0 %collective-permute-done.3.rb_ref = bf16[4,32,128]{2,1,0:T(8,128)(2,1)S(1)} collective-permute-done((bf16[4,32,128]{2,1,0:T(8,128)(2,1)S(1)}, bf16[4,32,128]{2,1,0:T(8,128)(2,1)S(1)}, u32[]{:S(2)}, u32[]{:S(2)}) %collective-permute-start.3) | collective-permute-done | bytes 32800 | tf_op jit(solution)/shard_map/ppermute | solution.py:431
  23.5 9.1 %shard_map.157 = (bf16[24,16,128]{2,1,0:T(8,128)(2,1)}, bf16[24,16,128]{2,1,0:T(8,128)(2,1)}, f32[4,128]{1,0:T(4,128)S(1)}) custom-call(f32[24,48,128]{2,1,0:T(8,128)S(1)} %get-tuple-element.38.val0, f32[24,48,128]{2,1,0:T(8,128)S(1)} %get-tuple-element.39.rew, f32[24,48,128]{2,1,0:T(8,128)S(1)} %get-tuple-element.40.sen, ...), custom_call_target="tpu_custom_call" | custom-call | tf_op jit(solution)/shard_map/pallas_call | solution.py:33
  32.6 15.6 %all_to_all.10 = f32[32,4,128]{2,1,0:T(4,128)S(1)} all-to-all(f32[32,4,128]{2,1,0:T(4,128)S(1)} %broadcast_in_dim.25), channel_id=1, replica_groups={{0,1,32,33,64,65,96,97,128,129,160,161,192,193,224,225,256,257,288,289,..., dimensions={0} | all-to-all | bytes 131072 | tf_op jit(solution)/shard_map/all_to_all | solution.py:437
  48.2 26.0 %all_to_all.11.refs_0_ = f32[16,4,128]{2,1,0:T(4,128)S(1)} all-to-all(f32[16,4,128]{2,1,0:T(4,128)S(1)} %broadcast_in_dim.26), channel_id=1, replica_groups={{0,2,4,6,8,10,12,14,16,18,20,22,24,26,28,30},{1,3,5,7,9,11,13,15,17,19,..., dimensions={0} | all-to-all | bytes 65536 | tf_op jit(solution)/shard_map/all_to_all | solution.py:437
  74.3 1.2 %shard_map.158 = (f32[16,64]{1,0:T(8,128)}, f32[64]{0:T(128)}, f32[64,64]{1,0:T(8,128)}, f32[64,64]{1,0:T(8,128)}, f32[24,64]{1,0:T(8,128)}) custom-call(f32[16,4,128]{2,1,0:T(4,128)S(1)} %all_to_all.11.refs_0_, s32[1,64]{1,0:T(1,128)S(1)} %get-tuple-element.51.refs_1_, f32[16,64]{1,0:T(8,128)S(1)} %get-tuple-element.52.refs_2_, ...), custom_call_target="tpu_custom_call" | custom-call | tf_op jit(solution)/shard_map/pallas_call | solution.py:33
  (8 shorter events, 0.1 us)
Async XLA Ops:
  2.4 6.2 %copy-start = (bf16[64,64]{1,0:T(8,128)(2,1)S(1)}, bf16[64,64]{1,0:T(8,128)(2,1)}, u32[]{:S(2)}) copy-start(bf16[64,64]{1,0:T(8,128)(2,1)} %w1_hbm.1) | copy-start | bytes 24580
  2.4 6.2 %copy-start.1 = (bf16[64,64]{1,0:T(8,128)(2,1)S(1)}, bf16[64,64]{1,0:T(8,128)(2,1)}, u32[]{:S(2)}) copy-start(bf16[64,64]{1,0:T(8,128)(2,1)} %w2_hbm.1) | copy-start | bytes 24580
  2.5 6.1 %copy-start.2 = (bf16[64,24]{0,1:T(8,128)(2,1)S(1)}, bf16[64,24]{0,1:T(8,128)(2,1)}, u32[]{:S(2)}) copy-start(bf16[64,24]{0,1:T(8,128)(2,1)} %param.19) | copy-start | bytes 9220
  2.6 7.2 %collective-permute-start = (bf16[24,16,128]{2,1,0:T(8,128)(2,1)S(1)}, bf16[24,16,128]{2,1,0:T(8,128)(2,1)S(1)}, u32[]{:S(2)}, u32[]{:S(2)}) collective-permute-start(bf16[24,16,128]{2,1,0:T(8,128)(2,1)S(1)} %get-tuple-element.35), channel_id=1, source_target_pairs={{0,32},{32,64},{64,96},{96,128},{128,160},{160,192},{192,224},{224... | collective-permute-start | bytes 294920 | tf_op jit(solution)/shard_map/ppermute | solution.py:431
  6.6 5.4 %collective-permute-start.1 = (bf16[24,16,128]{2,1,0:T(8,128)(2,1)S(1)}, bf16[24,16,128]{2,1,0:T(8,128)(2,1)S(1)}, u32[]{:S(2)}, u32[]{:S(2)}) collective-permute-start(bf16[24,16,128]{2,1,0:T(8,128)(2,1)S(1)} %get-tuple-element.36), channel_id=1, source_target_pairs={{32,0},{64,32},{96,64},{128,96},{160,128},{192,160},{224,192},{256... | collective-permute-start | bytes 294920 | tf_op jit(solution)/shard_map/ppermute | solution.py:431
  8.5 0.7 copy-start.3
  8.6 0.7 copy-start.4
  12.7 8.7 %collective-permute-start.2 = (bf16[4,32,128]{2,1,0:T(8,128)(2,1)S(1)}, bf16[4,32,128]{2,1,0:T(8,128)(2,1)S(1)}, u32[]{:S(2)}, u32[]{:S(2)}) collective-permute-start(bf16[4,32,128]{2,1,0:T(8,128)(2,1)S(1)} %get-tuple-element.46), channel_id=1, source_target_pairs={{0,1},{1,2},{2,3},{3,4},{4,5},{5,6},{6,7},{7,8},{8,9},{9,10},{10,1... | collective-permute-start | bytes 98312 | tf_op jit(solution)/shard_map/ppermute | solution.py:431
  18.2 5.2 %collective-permute-start.3 = (bf16[4,32,128]{2,1,0:T(8,128)(2,1)S(1)}, bf16[4,32,128]{2,1,0:T(8,128)(2,1)S(1)}, u32[]{:S(2)}, u32[]{:S(2)}) collective-permute-start(bf16[4,32,128]{2,1,0:T(8,128)(2,1)S(1)} %get-tuple-element.47), channel_id=1, source_target_pairs={{1,0},{2,1},{3,2},{4,3},{5,4},{6,5},{7,6},{8,7},{9,8},{10,9},{11,1... | collective-permute-start | bytes 98312 | tf_op jit(solution)/shard_map/ppermute | solution.py:431
